TPU v7x, 256 devices: a whole 4x4x8 slice. The times are simulated.
256 devices in a mesh: blk: 64 (over y, z, core), rep: 4 (over x).
Axes of the slice: x: 4, y: 4, z: 8, core: 2. Of those that a mesh axis runs over, the one named last changes fastest.
Arguments:
- embeddings: bfloat16 [98304, 1024], P('blk'), may hold values from -12 to 12
- pick: int32 [64, 64], replicated, may hold values from 0 to 6, as said below
- mask: int32 [64, 64, 6], replicated, may hold values from 0 to 1, as said below
Outputs:
- log_weight: float32 [384, 256], P('blk', 'rep')
Inputs may be any that keep to these rules, and one draw needn't show every extreme that they name: pick[k, k] = 6; a value of 6 means that owner k takes no block of owner p. mask[k, p, a] is 0 wherever pick[k, p] = 6, and is 1 for at least one a wherever pick[k, p] < 6.
All inputs are finite; a program needn't handle non-finite values.
Results may differ from a plain program's by a relative error of at most 0.0003.
Values may be sent and summed in bfloat16 or wider, within the bound.
A program may use at most 384 MiB of HBM per device.

v0:
```python
import math

import jax
import jax.numpy as jnp
from jax import lax
from jax.sharding import PartitionSpec as P

W = 1024
BR = 256
BLK_DEV = 6


MIN_SCORE = -1e30


def combine_pair(peak_a, total_a, peak_b, total_b):
    peak_new = jnp.maximum(peak_a, peak_b)
    return (peak_new, total_a * jnp.exp(peak_a - peak_new) + total_b * jnp.exp(peak_b - peak_new))


def tile_stats(left_block, right_rows, is_live, score_scale):
    scores = (
        jnp.einsum("iw,jw->ij", left_block, right_rows, preferred_element_type=jnp.float32)
        * score_scale
    )
    kept_scores = jnp.where(is_live[None, :], scores, MIN_SCORE)
    row_peak = jnp.max(kept_scores, axis=1)
    row_total = jnp.sum(
        jnp.where(is_live[None, :], jnp.exp(scores - row_peak[:, None]), 0.0), axis=1
    )
    col_raw = jnp.max(scores, axis=0)
    col_total = jnp.sum(jnp.exp(scores - col_raw[None, :]), axis=0)
    col_peak = jnp.where(is_live, col_raw, MIN_SCORE)
    col_total = jnp.where(is_live, col_total, 0.0)
    return (row_peak, row_total, col_peak, col_total)


def body(embeddings, pick, mask):
    owner_count = lax.axis_size("blk")
    rep_count = lax.axis_size("rep")
    my_owner = lax.axis_index("blk")
    my_rep = lax.axis_index("rep")
    quarter_rows = BR // rep_count
    score_scale = 1.0 / math.sqrt(W)
    blocks = embeddings.reshape(BLK_DEV, BR, W)
    quarters = lax.dynamic_slice_in_dim(blocks, my_rep * quarter_rows, quarter_rows, 1)
    column = pick[:, my_owner]
    pair_bits = mask[my_owner]
    row_index = jnp.arange(BR)[:, None]
    col_index = my_rep * quarter_rows + jnp.arange(quarter_rows)[None, :]
    self_mask = row_index == col_index
    own_scores = (
        jnp.einsum("aiw,ajw->aij", blocks, quarters, preferred_element_type=jnp.float32)
        * score_scale
    )
    own_scores = jnp.where(self_mask[None], MIN_SCORE, own_scores)
    own_peak = jnp.max(own_scores, axis=2)
    own_total = jnp.sum(jnp.exp(own_scores - own_peak[:, :, None]), axis=2)
    choose = jnp.minimum(column, BLK_DEV - 1)
    outgoing = jnp.take(quarters, choose, axis=0)
    outgoing = jnp.where((column < BLK_DEV)[:, None, None], outgoing, jnp.zeros_like(outgoing))
    incoming = lax.all_to_all(outgoing, "blk", split_axis=0, concat_axis=0, tiled=True)
    partners = incoming.reshape(owner_count * quarter_rows, W)
    peak_list = []
    total_list = []
    col_peak = jnp.full((owner_count * quarter_rows,), MIN_SCORE, jnp.float32)
    col_total = jnp.zeros((owner_count * quarter_rows,), jnp.float32)
    for local_id in range(BLK_DEV):
        is_live = jnp.repeat(pair_bits[:, local_id] == 1, quarter_rows)
        row_peak, row_total, tile_peak, tile_total = tile_stats(
            blocks[local_id], partners, is_live, score_scale
        )
        row_peak, row_total = combine_pair(
            own_peak[local_id], own_total[local_id], row_peak, row_total
        )
        peak_list.append(row_peak)
        total_list.append(row_total)
        col_peak, col_total = combine_pair(col_peak, col_total, tile_peak, tile_total)
    row_peak = jnp.stack(peak_list)
    row_total = jnp.stack(total_list)
    send_peak = col_peak.reshape(owner_count, quarter_rows)
    send_total = col_total.reshape(owner_count, quarter_rows)
    got_peak, got_total = (
        lax.all_to_all(send_peak, "blk", split_axis=0, concat_axis=0, tiled=True),
        lax.all_to_all(send_total, "blk", split_axis=0, concat_axis=0, tiled=True),
    )
    selected = column[:, None] == jnp.arange(BLK_DEV)[None, :]
    back_peak = jnp.max(jnp.where(selected[:, :, None], got_peak[:, None, :], MIN_SCORE), axis=0)
    back_total = jnp.sum(
        jnp.where(
            selected[:, :, None],
            got_total[:, None, :] * jnp.exp(got_peak[:, None, :] - back_peak[None]),
            0.0,
        ),
        axis=0,
    )
    peak_all = lax.pmax(row_peak, "rep")
    total_all = lax.psum(row_total * jnp.exp(row_peak - peak_all), "rep")
    quarter_peak = lax.dynamic_slice_in_dim(peak_all, my_rep * quarter_rows, quarter_rows, 1)
    quarter_total = lax.dynamic_slice_in_dim(total_all, my_rep * quarter_rows, quarter_rows, 1)
    final_peak, final_total = combine_pair(quarter_peak, quarter_total, back_peak, back_total)
    return final_peak + jnp.log(final_total)


def solution(mesh):
    return jax.shard_map(
        body,
        mesh=mesh,
        in_specs=(P("blk", None), P(), P()),
        out_specs=P("blk", "rep"),
        check_vma=False,
    )
```

profile of v0, /device:TPU:1, one launch (start us, length us, event | category | flops | bytes accessed | tf_op | source)
XLA Modules:
  0.0 333.2 jit_solution(14491932957121660254)
XLA Ops:
  0.0 1.0 and_reduce_fusion
  1.0 0.9 dynamic-slice_reduce_fusion
  2.0 1.2 constant_dynamic-slice_fusion.1
  3.2 5.5 %gather_fusion = bf16[64,64,1024]{2,1,0:T(8,128)(2,1)} fusion(bf16[6,64,1024]{2,1,0:T(8,128)(2,1)S(1)} %constant_dynamic-slice_fusion.1, s32[1024]{0:T(1024)S(1)} %pad_clamp_fusion), kind=kCustom, calls=%fused_computation | custom fusion | bytes 16777472 | tf_op jit(solution)/shard_map/jit(_take)/gather | solution.py:60
  8.6 7.6 %select_select_fusion = bf16[64,64,1024]{2,1,0:T(8,128)(2,1)} fusion(bf16[64,64,1024]{2,1,0:T(8,128)(2,1)} %gather_fusion, pred[64]{0:T(512)(128)(4,1)S(1)} %and_reduce_fusion, pred[64]{0:T(512)(128)(4,1)S(1)} %broadcast_compare_fusion), kind=kLoop, calls=%fused_computation.1 | loop fusion | flops 8388608 | bytes 16777344 | tf_op jit(solution)/shard_map/jit(_where)/select_n | solution.py:61
  16.3 13.3 %all-to-all-start = ((bf16[64,64,1024]{2,1,0:T(8,128)(2,1)}), bf16[64,64,1024]{2,1,0:T(8,128)(2,1)}, u32[]{:S(2)}, u32[]{:S(2)}) async-start(bf16[64,64,1024]{2,1,0:T(8,128)(2,1)} %select_select_fusion), calls=%async_computation | async-start | bytes 16777216 | tf_op jit(solution)/shard_map/all_to_all | solution.py:62
  29.7 0.5 copy-done.10
  30.2 0.1 broadcast_in_dim.240
  30.3 0.1 broadcast_in_dim.241
  30.4 0.1 broadcast_in_dim.237
  30.4 0.1 broadcast_in_dim.238
  30.5 0.1 broadcast_in_dim.234
  30.6 0.1 broadcast_in_dim.235
  30.7 0.1 broadcast_in_dim.231
  30.8 0.7 broadcast_in_dim.232
  31.5 0.1 broadcast_in_dim.228
  31.5 0.7 broadcast_in_dim.229
  32.2 0.1 broadcast_in_dim.220
  32.3 0.7 broadcast_in_dim.221
  33.0 0.1 iota_compare_fusion
  33.1 3.0 fusion.28
  36.1 0.1 exponential_reduce_fusion.6
  36.1 0.6 iota_compare_fusion.1
  36.7 178.6 %all-to-all-done = bf16[64,64,1024]{2,1,0:T(8,128)(2,1)} async-done(((bf16[64,64,1024]{2,1,0:T(8,128)(2,1)}), bf16[64,64,1024]{2,1,0:T(8,128)(2,1)}, u32[]{:S(2)}, u32[]{:S(2)}) %all-to-all-start) | async-done | bytes 8388640 | tf_op jit(solution)/shard_map/all_to_all | solution.py:62
  215.4 0.0 copy-done.20
  215.4 6.4 %select_reduce_fusion.6 = (f32[256]{0:T(256)S(1)}, f32[4096]{0:T(1024)S(1)}, f32[4096,256]{1,0:T(8,128)}) fusion(pred[4096]{0:T(1024)(128)(4,1)S(1)} %broadcast_in_dim.241, bf16[4096,1024]{1,0:T(8,128)(2,1)} %bitcast.4, bf16[1536,1024]{1,0:T(8,128)(2,1)} %param.3), kind=kOutput, calls=%fused_computation.20 | convolution fusion | flops 2151673600 | bytes 13128704 | tf_op jit(solution)/shard_map/iw,jw->ij/dot_general | solution.py:23
  221.8 0.1 reduce_max.174
  221.9 4.8 %select_reduce_fusion = (f32[256]{0:T(256)}, f32[4096]{0:T(1024)S(1)}) fusion(f32[4096,256]{1,0:T(8,128)} %get-tuple-element.56, f32[256]{0:T(256)S(1)} %get-tuple-element.7, pred[4096]{0:T(1024)(128)(4,1)S(1)} %broadcast_in_dim.241, f32[4096]{0:T(1024)S(1)} %get-tuple-element.8), kind=kLoop, calls=%fused_computation.14 | loop fusion | flops 5238528 | bytes 4233216 | tf_op jit(solution)/shard_map/reduce_sum | solution.py:28
  226.7 0.1 reduce_sum.174
  226.8 0.0 copy-done.1
  226.8 6.3 %select_reduce_fusion.7 = (f32[256]{0:T(256)S(1)}, f32[4096]{0:T(1024)S(1)}, f32[4096,256]{1,0:T(8,128)}) fusion(pred[4096]{0:T(1024)(128)(4,1)S(1)} %broadcast_in_dim.238, bf16[4096,1024]{1,0:T(8,128)(2,1)} %bitcast.4, bf16[1536,1024]{1,0:T(8,128)(2,1)S(1)} %copy-done.1), kind=kOutput, calls=%fused_computation.21 | convolution fusion | flops 2151673600 | bytes 13128704 | tf_op jit(solution)/shard_map/iw,jw->ij/dot_general | solution.py:23
  233.1 0.1 reduce_max.172
  233.2 4.6 %select_reduce_fusion.1 = (f32[256]{0:T(256)}, f32[4096]{0:T(1024)S(1)}) fusion(f32[4096,256]{1,0:T(8,128)} %get-tuple-element.51, f32[256]{0:T(256)S(1)} %get-tuple-element.11, pred[4096]{0:T(1024)(128)(4,1)S(1)} %broadcast_in_dim.238, f32[4096]{0:T(1024)S(1)} %get-tuple-element.12), kind=kLoop, calls=%fused_computation.15 | loop fusion | flops 5238528 | bytes 4233216 | tf_op jit(solution)/shard_map/reduce_sum | solution.py:28
  237.8 0.1 reduce_sum.172
  237.9 6.3 %select_reduce_fusion.8 = (f32[256]{0:T(256)S(1)}, f32[4096]{0:T(1024)S(1)}, f32[4096,256]{1,0:T(8,128)}) fusion(pred[4096]{0:T(1024)(128)(4,1)S(1)} %broadcast_in_dim.235, bf16[4096,1024]{1,0:T(8,128)(2,1)} %bitcast.4, bf16[1536,1024]{1,0:T(8,128)(2,1)S(1)} %copy-done.1), kind=kOutput, calls=%fused_computation.22 | convolution fusion | flops 2151673600 | bytes 13128704 | tf_op jit(solution)/shard_map/iw,jw->ij/dot_general | solution.py:23
  244.3 0.0 copy-done.24
  244.3 0.1 reduce_max.170
  244.3 4.6 %select_reduce_fusion.2 = (f32[256]{0:T(256)}, f32[4096]{0:T(1024)}) fusion(f32[4096,256]{1,0:T(8,128)} %get-tuple-element.52, f32[256]{0:T(256)S(1)} %get-tuple-element.15, pred[4096]{0:T(1024)(128)(4,1)S(1)} %broadcast_in_dim.235, f32[4096]{0:T(1024)S(1)} %get-tuple-element.16), kind=kLoop, calls=%fused_computation.16 | loop fusion | flops 5238528 | bytes 4233216 | tf_op jit(solution)/shard_map/reduce_sum | solution.py:28
  249.0 0.8 reduce_sum.170
  249.8 6.9 %select_reduce_fusion.9 = (f32[256]{0:T(256)}, f32[4096]{0:T(1024)}, f32[4096,256]{1,0:T(8,128)}) fusion(pred[4096]{0:T(1024)(128)(4,1)} %broadcast_in_dim.232, bf16[4096,1024]{1,0:T(8,128)(2,1)} %bitcast.4, bf16[1536,1024]{1,0:T(8,128)(2,1)S(1)} %copy-done.1), kind=kOutput, calls=%fused_computation.23 | convolution fusion | flops 2151673600 | bytes 13128704 | tf_op jit(solution)/shard_map/iw,jw->ij/dot_general | solution.py:23
  256.8 1.4 reduce_max.168
  258.2 4.7 %select_reduce_fusion.3 = (f32[256]{0:T(256)}, f32[4096]{0:T(1024)}) fusion(f32[4096,256]{1,0:T(8,128)} %get-tuple-element.53, f32[256]{0:T(256)} %get-tuple-element.19, pred[4096]{0:T(1024)(128)(4,1)} %broadcast_in_dim.232, f32[4096]{0:T(1024)} %get-tuple-element.20), kind=kLoop, calls=%fused_computation.17 | loop fusion | flops 5238528 | bytes 4233216 | tf_op jit(solution)/shard_map/reduce_sum | solution.py:28
  262.8 1.4 reduce_sum.168
  264.3 6.9 %select_reduce_fusion.10 = (f32[256]{0:T(256)}, f32[4096]{0:T(1024)}, f32[4096,256]{1,0:T(8,128)}) fusion(pred[4096]{0:T(1024)(128)(4,1)} %broadcast_in_dim.229, bf16[4096,1024]{1,0:T(8,128)(2,1)} %bitcast.4, bf16[1536,1024]{1,0:T(8,128)(2,1)S(1)} %copy-done.1), kind=kOutput, calls=%fused_computation.24 | convolution fusion | flops 2151673600 | bytes 13128704 | tf_op jit(solution)/shard_map/iw,jw->ij/dot_general | solution.py:23
  271.2 7.0 %select_reduce_fusion.11 = (f32[256]{0:T(256)}, f32[4096]{0:T(1024)}, f32[4096,256]{1,0:T(8,128)}) fusion(pred[4096]{0:T(1024)(128)(4,1)S(1)} %copy-done.7, bf16[4096,1024]{1,0:T(8,128)(2,1)} %bitcast.4, bf16[1536,1024]{1,0:T(8,128)(2,1)S(1)} %copy-done.1), kind=kOutput, calls=%fused_computation.25 | convolution fusion | flops 2151673600 | bytes 13128704 | tf_op jit(solution)/shard_map/iw,jw->ij/dot_general | solution.py:23
  278.2 0.9 reduce_max.166
  279.0 0.8 reduce_max.164
  279.8 0.0 copy-start.2
  279.9 0.0 copy-start.9
  279.9 0.0 copy-start.33
  280.0 4.2 %select_reduce_fusion.5 = (f32[256]{0:T(256)S(1)}, f32[4096]{0:T(1024)S(1)}) fusion(f32[4096,256]{1,0:T(8,128)} %get-tuple-element.55, f32[256]{0:T(256)} %get-tuple-element.27, pred[4096]{0:T(1024)(128)(4,1)} %broadcast_in_dim.221, f32[4096]{0:T(1024)} %get-tuple-element.28), kind=kLoop, calls=%fused_computation.19 | loop fusion | flops 5238528 | bytes 4233216 | tf_op jit(solution)/shard_map/reduce_sum | solution.py:28
  284.3 2.0 select_reduce_fusion.4
  286.5 8.6 %pmax.7 = f32[6,256]{1,0:T(8,128)S(1)} all-reduce(f32[6,256]{1,0:T(8,128)S(1)} %stack.4), channel_id=1, replica_groups=mesh['blk'=64,'rep'=4] {'rep'}, use_global_device_ids=true, to_apply=%region_7.8 | all-reduce | flops 1536 | bytes 12288 | tf_op jit(solution)/shard_map/pmax | solution.py:97
  295.1 0.1 reduce_sum.164
  295.2 0.1 reduce_sum.166
  295.4 1.6 multiply_add_fusion
  297.0 7.9 %all-to-all-start.1 = ((f32[64,1,64]{2,1,0:T(1,128)}), f32[64,1,64]{2,1,0:T(1,128)S(1)}, u32[]{:S(2)}, u32[]{:S(2)}) async-start(f32[64,1,64]{2,1,0:T(1,128)} %get-tuple-element.32), calls=%async_computation.1 | async-start | bytes 65536 | tf_op jit(solution)/shard_map/all_to_all | solution.py:84
  304.9 6.7 %psum.7 = f32[6,256]{1,0:T(8,128)S(1)} all-reduce(f32[6,256]{1,0:T(8,128)S(1)} %exponential_multiply_fusion), channel_id=1, replica_groups=mesh['blk'=64,'rep'=4] {'rep'}, use_global_device_ids=true, to_apply=%region_22.23 | all-reduce | flops 1536 | bytes 12288 | tf_op jit(solution)/shard_map/psum | solution.py:98
  311.6 2.5 all-to-all-done.1
  314.2 9.0 %all-to-all-start.2 = ((f32[64,1,64]{2,1,0:T(1,128)}), f32[64,1,64]{2,1,0:T(1,128)S(1)}, u32[]{:S(2)}, u32[]{:S(2)}) async-start(f32[64,1,64]{2,1,0:T(1,128)} %get-tuple-element.31), calls=%async_computation.2 | async-start | bytes 65536 | tf_op jit(solution)/shard_map/all_to_all | solution.py:85
  323.1 0.1 select_reduce_fusion.13
  323.3 9.1 %all-to-all-done.2 = f32[64,1,64]{2,1,0:T(1,128)S(1)} async-done(((f32[64,1,64]{2,1,0:T(1,128)}), f32[64,1,64]{2,1,0:T(1,128)S(1)}, u32[]{:S(2)}, u32[]{:S(2)}) %all-to-all-start.2) | async-done | bytes 16416 | tf_op jit(solution)/shard_map/all_to_all | solution.py:85
  332.4 0.1 select_reduce_fusion.12
  332.5 0.7 log_add_fusion
  (72 shorter events, 0.3 us)
Async XLA Ops:
  0.0 29.6 %copy-start = (s32[64,64,6]{1,0,2:T(8,128)S(1)}, s32[64,64,6]{1,0,2:T(8,128)}, u32[]{:S(2)}) copy-start(s32[64,64,6]{1,0,2:T(8,128)} %param.5) | copy-start | bytes 294916
  16.3 199.1 %all-to-all-start = ((bf16[64,64,1024]{2,1,0:T(8,128)(2,1)}), bf16[64,64,1024]{2,1,0:T(8,128)(2,1)}, u32[]{:S(2)}, u32[]{:S(2)}) async-start(bf16[64,64,1024]{2,1,0:T(8,128)(2,1)} %select_select_fusion), calls=%async_computation | async-start | bytes 16777216 | tf_op jit(solution)/shard_map/all_to_all | solution.py:62
  29.7 0.5 copy-start.10
  29.7 3.3 copy-start.12
  29.7 3.3 copy-start.14
  29.7 185.7 %copy-start.16 = (pred[64]{0:T(512)(128)(4,1)}, pred[64]{0:T(512)(128)(4,1)S(1)}, u32[]{:S(2)}) copy-start(pred[64]{0:T(512)(128)(4,1)S(1)} %get-tuple-element.48) | copy-start | bytes 196
  29.7 185.7 %copy-start.18 = (pred[64]{0:T(512)(128)(4,1)}, pred[64]{0:T(512)(128)(4,1)S(1)}, u32[]{:S(2)}) copy-start(pred[64]{0:T(512)(128)(4,1)S(1)} %get-tuple-element.49) | copy-start | bytes 196
  29.7 185.7 %copy-start.20 = (pred[64]{0:T(512)(128)(4,1)}, pred[64]{0:T(512)(128)(4,1)S(1)}, u32[]{:S(2)}) copy-start(pred[64]{0:T(512)(128)(4,1)S(1)} %get-tuple-element.50) | copy-start | bytes 196
  221.8 11.3 %copy-start.8 = (f32[256]{0:T(256)}, f32[256]{0:T(256)S(1)}, u32[]{:S(2)}) copy-start(f32[256]{0:T(256)S(1)} %get-tuple-element.7) | copy-start | bytes 3076
  221.8 5.0 %copy-start.1 = (bf16[1536,1024]{1,0:T(8,128)(2,1)S(1)}, bf16[1536,1024]{1,0:T(8,128)(2,1)}, u32[]{:S(2)}) copy-start(bf16[1536,1024]{1,0:T(8,128)(2,1)} %param.3) | copy-start | bytes 9437188
  233.1 11.1 %copy-start.24 = (f32[256]{0:T(256)}, f32[256]{0:T(256)S(1)}, u32[]{:S(2)}) copy-start(f32[256]{0:T(256)S(1)} %get-tuple-element.11) | copy-start | bytes 3076
  244.3 4.7 %copy-start.27 = (f32[256]{0:T(256)}, f32[256]{0:T(256)S(1)}, u32[]{:S(2)}) copy-start(f32[256]{0:T(256)S(1)} %get-tuple-element.15) | copy-start | bytes 3076
  264.2 6.9 %copy-start.7 = (pred[4096]{0:T(1024)(128)(4,1)S(1)}, pred[4096]{0:T(1024)(128)(4,1)}, u32[]{:S(2)}) copy-start(pred[4096]{0:T(1024)(128)(4,1)} %broadcast_in_dim.221) | copy-start | bytes 12292
  278.2 6.1 %copy-start.5 = (f32[4096]{0:T(1024)S(1)}, f32[4096]{0:T(1024)}, u32[]{:S(2)}) copy-start(f32[4096]{0:T(1024)} %get-tuple-element.24) | copy-start | bytes 49156
  278.2 6.1 %copy-start.6 = (pred[4096]{0:T(1024)(128)(4,1)S(1)}, pred[4096]{0:T(1024)(128)(4,1)}, u32[]{:S(2)}) copy-start(pred[4096]{0:T(1024)(128)(4,1)} %broadcast_in_dim.229) | copy-start | bytes 12292
  278.2 6.1 %copy-start.32 = (f32[256]{0:T(256)S(1)}, f32[256]{0:T(256)}, u32[]{:S(2)}) copy-start(f32[256]{0:T(256)} %get-tuple-element.23) | copy-start | bytes 3076
  279.8 4.5 %copy-start.2 = (f32[4096,256]{1,0:T(8,128)S(1)}, f32[4096,256]{1,0:T(8,128)}, u32[]{:S(2)}) copy-start(f32[4096,256]{1,0:T(8,128)} %get-tuple-element.54) | copy-start | bytes 12582916
  279.9 6.5 %copy-start.9 = (f32[256]{0:T(256)S(1)}, f32[256]{0:T(256)}, u32[]{:S(2)}) copy-start(f32[256]{0:T(256)} %copy-done.8) | copy-start | bytes 3076
  279.9 6.5 %copy-start.33 = (f32[256]{0:T(256)S(1)}, f32[256]{0:T(256)}, u32[]{:S(2)}) copy-start(f32[256]{0:T(256)} %get-tuple-element.27) | copy-start | bytes 3076
  279.9 6.5 %copy-start.23 = (f32[256]{0:T(256)S(1)}, f32[256]{0:T(256)}, u32[]{:S(2)}) copy-start(f32[256]{0:T(256)} %get-tuple-element.5) | copy-start | bytes 3076
  279.9 6.5 %copy-start.25 = (f32[256]{0:T(256)S(1)}, f32[256]{0:T(256)}, u32[]{:S(2)}) copy-start(f32[256]{0:T(256)} %copy-done.24) | copy-start | bytes 3076
  279.9 6.5 %copy-start.26 = (f32[256]{0:T(256)S(1)}, f32[256]{0:T(256)}, u32[]{:S(2)}) copy-start(f32[256]{0:T(256)} %get-tuple-element.9) | copy-start | bytes 3076
  279.9 6.5 %copy-start.28 = (f32[256]{0:T(256)S(1)}, f32[256]{0:T(256)}, u32[]{:S(2)}) copy-start(f32[256]{0:T(256)} %copy-done.27) | copy-start | bytes 3076
  279.9 6.5 %copy-start.29 = (f32[256]{0:T(256)S(1)}, f32[256]{0:T(256)}, u32[]{:S(2)}) copy-start(f32[256]{0:T(256)} %get-tuple-element.13) | copy-start | bytes 3076
  279.9 6.5 %copy-start.30 = (f32[256]{0:T(256)S(1)}, f32[256]{0:T(256)}, u32[]{:S(2)}) copy-start(f32[256]{0:T(256)} %get-tuple-element.19) | copy-start | bytes 3076
  279.9 6.5 %copy-start.31 = (f32[256]{0:T(256)S(1)}, f32[256]{0:T(256)}, u32[]{:S(2)}) copy-start(f32[256]{0:T(256)} %get-tuple-element.17) | copy-start | bytes 3076
  279.9 15.3 %copy-start.3 = (f32[64,1,64]{2,1,0:T(1,128)S(1)}, f32[64,1,64]{2,1,0:T(1,128)}, u32[]{:S(2)}) copy-start(f32[64,1,64]{2,1,0:T(1,128)} %reduce_max.168) | copy-start | bytes 49156
  280.0 15.3 %copy-start.4 = (f32[64,1,64]{2,1,0:T(1,128)S(1)}, f32[64,1,64]{2,1,0:T(1,128)}, u32[]{:S(2)}) copy-start(f32[64,1,64]{2,1,0:T(1,128)} %reduce_sum.168) | copy-start | bytes 49156
  280.0 15.3 %copy-start.11 = (pred[64]{0:T(512)(128)(4,1)S(1)}, pred[64]{0:T(512)(128)(4,1)}, u32[]{:S(2)}) copy-start(pred[64]{0:T(512)(128)(4,1)} %copy-done.10) | copy-start | bytes 196
  280.0 15.3 %copy-start.13 = (pred[64]{0:T(512)(128)(4,1)S(1)}, pred[64]{0:T(512)(128)(4,1)}, u32[]{:S(2)}) copy-start(pred[64]{0:T(512)(128)(4,1)} %copy-done.12) | copy-start | bytes 196
  280.0 15.3 %copy-start.15 = (pred[64]{0:T(512)(128)(4,1)S(1)}, pred[64]{0:T(512)(128)(4,1)}, u32[]{:S(2)}) copy-start(pred[64]{0:T(512)(128)(4,1)} %copy-done.14) | copy-start | bytes 196
  280.0 15.3 %copy-start.17 = (pred[64]{0:T(512)(128)(4,1)S(1)}, pred[64]{0:T(512)(128)(4,1)}, u32[]{:S(2)}) copy-start(pred[64]{0:T(512)(128)(4,1)} %copy-done.16) | copy-start | bytes 196
  280.0 15.3 %copy-start.19 = (pred[64]{0:T(512)(128)(4,1)S(1)}, pred[64]{0:T(512)(128)(4,1)}, u32[]{:S(2)}) copy-start(pred[64]{0:T(512)(128)(4,1)} %copy-done.18) | copy-start | bytes 196
  280.0 15.3 %copy-start.21 = (pred[64]{0:T(512)(128)(4,1)S(1)}, pred[64]{0:T(512)(128)(4,1)}, u32[]{:S(2)}) copy-start(pred[64]{0:T(512)(128)(4,1)} %copy-done.20) | copy-start | bytes 196
  280.0 43.1 %copy-start.22 = (pred[64,6]{0,1:T(8,128)(4,1)S(1)}, pred[64,6]{0,1:T(8,128)(4,1)}, u32[]{:S(2)}) copy-start(pred[64,6]{0,1:T(8,128)(4,1)} %iota_compare_fusion.1) | copy-start | bytes 1156
  297.0 17.2 %all-to-all-start.1 = ((f32[64,1,64]{2,1,0:T(1,128)}), f32[64,1,64]{2,1,0:T(1,128)S(1)}, u32[]{:S(2)}, u32[]{:S(2)}) async-start(f32[64,1,64]{2,1,0:T(1,128)} %get-tuple-element.32), calls=%async_computation.1 | async-start | bytes 65536 | tf_op jit(solution)/shard_map/all_to_all | solution.py:84
  314.2 18.3 %all-to-all-start.2 = ((f32[64,1,64]{2,1,0:T(1,128)}), f32[64,1,64]{2,1,0:T(1,128)S(1)}, u32[]{:S(2)}, u32[]{:S(2)}) async-start(f32[64,1,64]{2,1,0:T(1,128)} %get-tuple-element.31), calls=%async_computation.2 | async-start | bytes 65536 | tf_op jit(solution)/shard_map/all_to_all | solution.py:85
where the time goes:
time: 334 us; the launch traced here: 333 us
  waiting for transfers between devices  190 us (57%)
  matrix products  42.9 us (13%)
  other arithmetic  37.9 us (11%)
  starting transfers between devices  30.2 us (9%)
  local copies, waits for them, and re-layouts  16 us (5%)
  blocking collectives  15.3 us (5%)
    all_to_all x1, waiting for transfers between devices, body(): lax.all_to_all(outgoing, 'blk', split_axis=0, concat_axis=0, tiled=True)  179 us
    dot_general x6, matrix products, tile_stats(): jnp.einsum('iw,jw->ij', left_block, right_rows, preferred_element_type=jn...  40 us
    reduce_sum x6, other arithmetic, tile_stats(): jnp.sum(jnp.where(is_live[None, :], jnp.exp(scores - row_peak[:, None]),...  25 us
    all_to_all x1, starting transfers between devices, body(): lax.all_to_all(outgoing, 'blk', split_axis=0, concat_axis=0, tiled=True)  13.3 us
    all_to_all x1, waiting for transfers between devices, body(): lax.all_to_all(send_total, 'blk', split_axis=0, concat_axis=0, tiled=True)  9.14 us
    all_to_all x1, starting transfers between devices, body(): lax.all_to_all(send_total, 'blk', split_axis=0, concat_axis=0, tiled=True)  8.96 us
    pmax x1, blocking collectives, body(): peak_all = lax.pmax(row_peak, 'rep')  8.58 us
    all_to_all x1, starting transfers between devices, body(): lax.all_to_all(send_peak, 'blk', split_axis=0, concat_axis=0, tiled=True)  7.92 us
  transfers between devices with their start and end apart: 3, of which 3 were waited for; matrix products, arithmetic and copies ran while one was open for 2% of the time, Pallas kernels for 0%

commit v1 on v0

v1 whole, which is shorter than its diff:
```python
import math

import jax
import jax.numpy as jnp
from jax import lax
from jax.experimental import pallas as pl
from jax.experimental.pallas import tpu as pltpu
from jax.sharding import PartitionSpec as P

W = 1024
BR = 256
BLK_DEV = 6
NY, NZ, NC, NX = 4, 8, 2, 4
PLANE = NY * NC
Q = BR // NX
COLS = PLANE * Q
SLOTS = NZ
LOW = -1e30
TO_BASE2 = math.log2(math.e) / math.sqrt(W)
LN2 = math.log(2.0)
NT = (((1,), (1,)), ((), ()))


def kernel(
    emb, pick, bias, pcol, out,
    q0, ra1, ra2, ra3, rb1, rb2, rb3, r4, staged, held, row_max, row_sum, col_max, col_sum,
    col_send, col_mid, col_turn, col_got, row_send, row_got,
    z_send, z_recv, y_send, y_recv, cy_send, cy_recv, cz_send, cz_recv, x_send, x_recv,
):
    me = lax.axis_index("blk")
    x = lax.axis_index("rep")
    c = lax.rem(me, NC)
    z = lax.rem(me // NC, NZ)
    y = me // (NC * NZ)

    def blk_id(yy, zz, cc):
        return (yy * NZ + zz) * NC + cc

    def z_peer(dz):
        return blk_id(y, lax.rem(z + dz + NZ, NZ), c)

    def plane_peer(j):
        return lax.rem(y + j // NC, NY), lax.rem(c + j % NC, NC)

    def send(src, dst, ssem, rsem, target):
        copy = pltpu.make_async_remote_copy(
            src_ref=src, dst_ref=dst, send_sem=ssem, recv_sem=rsem,
            device_id=target, device_id_type=pl.DeviceIdType.MESH,
        )
        copy.start()
        return copy

    barrier = pltpu.get_barrier_semaphore()
    for dz in range(1, NZ):
        pl.semaphore_signal(barrier, inc=1, device_id={"blk": z_peer(dz)}, device_id_type=pl.DeviceIdType.MESH)
    for j in range(1, PLANE):
        yy, cc = plane_peer(j)
        pl.semaphore_signal(barrier, inc=1, device_id={"blk": blk_id(yy, z, cc)}, device_id_type=pl.DeviceIdType.MESH)
    for dx in range(1, NX):
        pl.semaphore_signal(barrier, inc=1, device_id={"rep": lax.rem(x + dx, NX)}, device_id_type=pl.DeviceIdType.MESH)

    for a in range(BLK_DEV):
        q0[a] = emb[pl.ds(a * BR + x * Q, Q), :]
    pl.semaphore_wait(barrier, NZ - 1 + PLANE - 1 + NX - 1)

    pending = []
    ring_a = [q0, ra1, ra2, ra3]
    ring_b = [q0, rb1, rb2, rb3]
    right, left = {"blk": z_peer(1)}, {"blk": z_peer(-1)}
    half = BLK_DEV // 2

    def push_ring(d):
        if d < 3:
            a = send(ring_a[d], ring_a[d + 1], z_send.at[0, d], z_recv.at[0, d], right)
            b = send(ring_b[d], ring_b[d + 1], z_send.at[1, d], z_recv.at[1, d], left)
        else:
            a = send(ring_a[3].at[pl.ds(0, half)], r4.at[pl.ds(0, half)], z_send.at[0, 3], z_recv.at[0, 3], right)
            b = send(ring_b[3].at[pl.ds(half, half)], r4.at[pl.ds(half, half)], z_send.at[1, 3], z_recv.at[1, 3], left)
        pending.extend([a, b])
        return a, b

    plane_copies = {}

    def stage(slot, ring_ref, zz):
        owner = blk_id(y, zz, c)
        for j in [*range(1, PLANE), 0]:
            yy, cc = plane_peer(j)
            chosen = jnp.clip(pick[blk_id(yy, z, cc), owner], 0, BLK_DEV - 1)
            rows = ring_ref[chosen]
            if j == 0:
                held[zz, y * NC + c] = rows
            else:
                staged[slot, j - 1] = rows
                copy = send(
                    staged.at[slot, j - 1], held.at[zz, y * NC + c],
                    y_send.at[slot, j - 1], y_recv.at[slot, j - 1], {"blk": blk_id(yy, z, cc)},
                )
                plane_copies[slot, j] = copy
                pending.append(copy)

    def own_block(a, carry):
        base = pl.multiple_of(a * BR, BR)
        top = pl.multiple_of((x // 2) * (2 * Q), 2 * Q)
        scores = lax.dot_general(
            emb[pl.ds(base, BR), :], emb[pl.ds(base + top, 2 * Q), :], NT,
            preferred_element_type=jnp.float32,
        ) * TO_BASE2
        row = lax.broadcasted_iota(jnp.int32, (BR, 2 * Q), 0)
        col = lax.broadcasted_iota(jnp.int32, (BR, 2 * Q), 1) + top
        valid = (col // Q == x) & (row != col)
        row_max[a] = jnp.where(valid, scores, LOW)
        row_sum[a] = jnp.where(valid, 1.0, 0.0)
        return carry

    def compute(slot, zz):
        for j in range(1, PLANE):
            plane_copies[slot, j].wait_recv()
        col_max[...] = jnp.full_like(col_max, LOW)
        col_sum[...] = jnp.zeros_like(col_sum)

        def one(a, carry):
            base = pl.multiple_of(a * BR, BR)
            t = lax.dot_general(
                emb[pl.ds(base, BR), :], held[zz].reshape(COLS, W), NT,
                preferred_element_type=jnp.float32,
            ) * TO_BASE2 + bias[zz, a]
            parts = [t[:, g * 128:(g + 1) * 128] for g in range(COLS // 128)]
            old = row_max[a]
            new = old
            for part in parts:
                new = jnp.maximum(new, part)
            total = row_sum[a] * jnp.exp2(old - new)
            for part in parts:
                total += jnp.exp2(part - new)
            row_max[a] = new
            row_sum[a] = total
            t8 = t.reshape(BR // 8, 8, COLS)
            old = col_max[...]
            new = jnp.maximum(old, jnp.max(t8, axis=0))
            col_sum[...] = col_sum[...] * jnp.exp2(old - new) + jnp.sum(jnp.exp2(t8 - new[None]), axis=0)
            col_max[...] = new
            return carry

        lax.fori_loop(0, BLK_DEV, one, 0)
        peak = jnp.max(col_max[...], axis=0, keepdims=True)
        total = jnp.sum(col_sum[...] * jnp.exp2(col_max[...] - peak), axis=0, keepdims=True)
        lse = peak + jnp.log2(total)
        for yy in range(NY):
            col_send[yy, pl.ds(zz, 1), :] = lse[:, yy * 128:(yy + 1) * 128]

    def zat(dz):
        return lax.rem(z + dz + NZ, NZ)

    ring = push_ring(0)
    stage(0, q0, z)
    lax.fori_loop(0, BLK_DEV, own_block, 0)
    ready = [(0, z)]
    for d in range(1, 4):
        ring[0].wait_recv()
        ring[1].wait_recv()
        ring = push_ring(d)
        stage(2 * d - 1, ring_a[d], zat(-d))
        stage(2 * d, ring_b[d], zat(d))
        for slot, zz in ready:
            compute(slot, zz)
        ready = [(2 * d - 1, zat(-d)), (2 * d, zat(d))]
    ring[0].wait_recv()
    ring[1].wait_recv()
    stage(7, r4, zat(4))
    for slot, zz in [*ready, (7, zat(4))]:
        compute(slot, zz)

    back = []
    for j in range(1, PLANE):
        yy, cc = plane_peer(j)
        back.append(send(
            col_send.at[yy], col_mid.at[y * NC + c], cy_send.at[j - 1], cy_recv.at[j - 1],
            {"blk": blk_id(yy, z, cc)},
        ))
    col_mid[y * NC + c] = col_send[y]

    row_send[...] = jnp.full_like(row_send, LOW)
    for a in range(BLK_DEV):
        m = row_max[a].T
        s = row_sum[a].T
        peak = jnp.max(m, axis=0, keepdims=True)
        lse = peak + jnp.log2(jnp.sum(s * jnp.exp2(m - peak), axis=0, keepdims=True))
        for h in range(2):
            row_send[h, a:a + 1, :] = lse[:, h * 128:(h + 1) * 128]
    across = []
    for dx in range(1, NX):
        xx = lax.rem(x + dx, NX)
        across.append(send(row_send.at[xx // 2], row_got.at[x], x_send.at[dx - 1], x_recv.at[dx - 1], {"rep": xx}))
    row_got[x] = row_send[x // 2]

    for copy in back:
        copy.wait_recv()
    for zz in range(NZ):
        for s in range(PLANE):
            col_turn[zz, s:s + 1, :] = col_mid[s, zz:zz + 1, :]
    final = []
    for dz in range(1, NZ):
        zz = zat(dz)
        final.append(send(
            col_turn.at[zz], col_got.at[z], cz_send.at[dz - 1], cz_recv.at[dz - 1], {"blk": blk_id(y, zz, c)}
        ))
    col_got[z] = col_turn[z]
    for copy in across:
        copy.wait_recv()
    for copy in final:
        copy.wait_recv()

    def to_front(v, shift_it):
        return jnp.where(shift_it, pltpu.roll(v, 64, 1), v)

    got = col_got[...].reshape(NZ * PLANE, 128)
    who = pcol[...].reshape(NZ * PLANE, 128)
    for b in range(BLK_DEV):
        chosen = who == b
        v = jnp.where(chosen, got, LOW)
        peak = jnp.max(v, axis=0, keepdims=True)
        total = jnp.sum(jnp.where(chosen, jnp.exp2(v - peak), 0.0), axis=0, keepdims=True)
        col_max[b:b + 1, 0:128] = peak
        col_sum[b:b + 1, 0:128] = total
    col_peak = to_front(col_max[:, 0:128], c == 1)
    col_total = to_front(col_sum[:, 0:128], c == 1)
    rows = [to_front(row_got[i], lax.rem(x, 2) == 1) for i in range(NX)]
    peak = col_peak
    for r in rows:
        peak = jnp.maximum(peak, r)
    total = col_total * jnp.exp2(col_peak - peak)
    for r in rows:
        total += jnp.exp2(r - peak)
    result = (peak + jnp.log2(total)) * LN2
    out[...] = result[:BLK_DEV, :Q]
    for copy in [*pending, *back, *across, *final]:
        copy.wait_send()


def body(embeddings, pick, mask):
    me = lax.axis_index("blk")
    live = mask[me].reshape(NY, NZ, NC, BLK_DEV).transpose(1, 3, 0, 2)
    bias = jnp.where(live == 1, 0.0, LOW).astype(jnp.float32)
    bias = jnp.broadcast_to(bias[..., None], (NZ, BLK_DEV, NY, NC, Q)).reshape(NZ, BLK_DEV, 1, COLS)
    pcol = pick[:, me].reshape(NY, NZ, NC).transpose(1, 0, 2).reshape(NZ, PLANE, 1)
    pcol = jnp.broadcast_to(pcol, (NZ, PLANE, 128))
    vmem = pl.BlockSpec(memory_space=pltpu.VMEM)
    dma = pltpu.SemaphoreType.DMA
    slab = pltpu.VMEM((BLK_DEV, Q, W), jnp.bfloat16)
    f32 = jnp.float32
    return pl.pallas_call(
        kernel,
        out_shape=jax.ShapeDtypeStruct((BLK_DEV, Q), f32),
        in_specs=[vmem, pl.BlockSpec(memory_space=pltpu.SMEM), vmem, vmem],
        out_specs=vmem,
        scratch_shapes=[
            *[slab] * 8,
            pltpu.VMEM((SLOTS, PLANE - 1, Q, W), jnp.bfloat16),
            pltpu.VMEM((NZ, PLANE, Q, W), jnp.bfloat16),
            pltpu.VMEM((BLK_DEV, BR, 128), f32),
            pltpu.VMEM((BLK_DEV, BR, 128), f32),
            pltpu.VMEM((8, COLS), f32),
            pltpu.VMEM((8, COLS), f32),
            pltpu.VMEM((NY, NZ, 128), f32),
            pltpu.VMEM((PLANE, NZ, 128), f32),
            pltpu.VMEM((NZ, PLANE, 128), f32),
            pltpu.VMEM((NZ, PLANE, 128), f32),
            pltpu.VMEM((2, 8, 128), f32),
            pltpu.VMEM((NX, 8, 128), f32),
            dma((2, 4)), dma((2, 4)),
            dma((SLOTS, PLANE - 1)), dma((SLOTS, PLANE - 1)),
            dma((PLANE - 1,)), dma((PLANE - 1,)),
            dma((NZ - 1,)), dma((NZ - 1,)),
            dma((NX - 1,)), dma((NX - 1,)),
        ],
        compiler_params=pltpu.CompilerParams(
            collective_id=0, has_side_effects=True, vmem_limit_bytes=56 * 1024 * 1024
        ),
        cost_estimate=pl.CostEstimate(
            flops=2 * 1536 * 4096 * W, bytes_accessed=8 * 1024 * 1024, transcendentals=2 * 1536 * 4096
        ),
    )(embeddings, pick, bias, pcol)


def solution(mesh):
    return jax.shard_map(
        body,
        mesh=mesh,
        in_specs=(P("blk", None), P(), P()),
        out_specs=P("blk", "rep"),
        check_vma=False,
    )
```

time: 334 us -> 129 us (0.39)
  waiting for transfers between devices: 190 us -> 0 us
  Pallas kernels: 0 us -> 123 us
  matrix products: 42.9 us -> 0 us
  other arithmetic: 37.9 us -> 0.74 us
  starting transfers between devices: 30.2 us -> 0 us
  blocking collectives: 15.3 us -> 0 us
  local copies, waits for them, and re-layouts: 16 us -> 4.68 us
    all_to_all x3 -> x0, waiting for transfers between devices: 190 us -> none  [the longest x1 179 us: body(): lax.all_to_all(outgoing, 'blk', split_axis=0, concat_axis=0, tiled=True)]
    pallas_call x0 -> x1, Pallas kernels: none -> 123 us  [body(): pl.pallas_call(kernel, out_shape=jax.ShapeDtypeStruct((BLK_DEV, Q), f32),...]
    dot_general x7 -> x0, matrix products: 42.9 us -> none  [the longest x6 40 us: tile_stats(): jnp.einsum('iw,jw->ij', left_block, right_rows, preferred_element_type=jn...]
    all_to_all x3 -> x0, starting transfers between devices: 30.2 us -> none  [the longest x1 13.3 us: body(): lax.all_to_all(outgoing, 'blk', split_axis=0, concat_axis=0, tiled=True)]
    reduce_sum x8 -> x0, other arithmetic: 25.2 us -> none  [the longest x6 25 us: tile_stats(): jnp.sum(jnp.where(is_live[None, :], jnp.exp(scores - row_peak[:, None]),...]
    pmax x1 -> x0, blocking collectives: 8.58 us -> none  [body(): peak_all = lax.pmax(row_peak, 'rep')]
    select_n x1, other arithmetic: 7.6 us -> 0.74 us  [body(): bias = jnp.where(live == 1, 0.0, LOW).astype(jnp.float32)]
    psum x1 -> x0, blocking collectives: 6.7 us -> none  [body(): total_all = lax.psum(row_total * jnp.exp(row_peak - peak_all), 'rep')]
  transfers between devices with their start and end apart: 3 -> 0, of which waited for: 3 -> 0; matrix products, arithmetic and copies ran while one was open for 2% -> 0% of each run, Pallas kernels for 0% -> 0%
where the time goes in v1:
time: 129 us
  Pallas kernels  123 us (95%)
  local copies, waits for them, and re-layouts  4.68 us (4%)
    pallas_call x1, Pallas kernels, body(): pl.pallas_call(kernel, out_shape=jax.ShapeDtypeStruct((BLK_DEV, Q), f32),...  123 us

profile of v1, /device:TPU:1, one launch (start us, length us, event | category | flops | bytes accessed | tf_op | source)
XLA Modules:
  0.0 128.9 jit_solution(10274209987511599337)
XLA Ops:
  0.0 0.7 compare_select_fusion
  0.7 0.1 copy.7
  0.8 0.3 copy.8
  1.2 0.3 broadcast_in_dim.23
  1.4 0.8 reshape.11.bias
  2.3 0.9 dynamic-slice_reduce_fusion
  3.2 0.1 reshape_squeeze.4
  3.3 0.1 copy.9
  3.4 0.1 copy.10
  3.5 0.7 broadcast_in_dim.25.pcol
  4.2 123.5 %shard_map.37 = f32[6,64]{1,0:T(8,128)} custom-call(bf16[1536,1024]{1,0:T(8,128)(2,1)} %emb.1, s32[64,64]{1,0:T(8,128)} %pick.1, f32[8,6,1,512]{3,2,1,0:T(1,128)} %reshape.11.bias, s32[8,8,128]{2,1,0:T(8,128)} %broadcast_in_dim.25.pcol), custom_call_target="tpu_custom_call" | custom-call | flops 12884901888 | bytes 8388608 | tf_op jit(solution)/shard_map/pallas_call | solution.py:251
  127.7 1.3 copy.12

commit v2 on v1

v2 whole, which is shorter than its diff:
```python
import math

import jax
import jax.numpy as jnp
from jax import lax
from jax.experimental import pallas as pl
from jax.experimental.pallas import tpu as pltpu
from jax.sharding import PartitionSpec as P

W = 1024
BR = 256
BLK_DEV = 6
NY, NZ, NC, NX = 4, 8, 2, 4
PLANE = NY * NC
Q = BR // NX
LANES = NC * Q
NEAR = 3
COLS_A = NEAR * LANES
COLS_F = NX * LANES
LOW = -1e30
TO_BASE2 = math.log2(math.e) / math.sqrt(W)
LN2 = math.log(2.0)
NT = (((1,), (1,)), ((), ()))
MESH = pl.DeviceIdType.MESH
NEAR_DY = (0, 1, NY - 1)
SEEN_AS = (0, 2, 1)


def kernel(
    emb, pick, mask, out,
    q0, ra1, ra2, ra3, rb1, rb2, rb3, r4, g2, emb_v, staged_a, staged_f, held_a, held_f,
    bits, bits_wide, bias_a, bias_f, pcol, row_max, row_sum, far_max, far_sum, far_t, col_max, col_sum,
    col_send_a, col_send_f, col_mid, col_far, col_turn, col_got, row_send, row_got, far_send, far_got,
    in_sem, z_send, z_recv, g_send, g_recv, a_send, a_recv, f_send, f_recv, w_send, w_recv,
    ca_send, ca_recv, cf_send, cf_recv, cz_send, cz_recv, x_send, x_recv, rf_send, rf_recv,
):
    me = lax.axis_index("blk")
    x = lax.axis_index("rep")
    c = lax.rem(me, NC)
    z = lax.rem(me // NC, NZ)
    y = me // (NC * NZ)
    other = 1 - c

    def blk_id(yy, zz, cc):
        return (yy * NZ + zz) * NC + cc

    def zat(dz):
        return lax.rem(z + dz + NZ, NZ)

    def yat(dy):
        return lax.rem(y + dy, NY)

    def xat(dx):
        return lax.rem(x + dx, NX)

    def at(yy, zz, cc, xx):
        return {"blk": blk_id(yy, zz, cc), "rep": xx}

    def core(k):
        return c if k == 0 else other

    far = blk_id(yat(2), z, c)
    far_device = at(yat(2), z, c, x)

    pending = []

    def send(src, dst, ssem, rsem, target):
        copy = pltpu.make_async_remote_copy(
            src_ref=src, dst_ref=dst, send_sem=ssem, recv_sem=rsem, device_id=target, device_id_type=MESH,
        )
        copy.start()
        pending.append(copy)
        return copy

    load_q = pltpu.make_async_copy(emb.at[:, pl.ds(x * Q, Q), :], q0, in_sem.at[0])
    load_e = pltpu.make_async_copy(emb, emb_v, in_sem.at[1])
    load_m = pltpu.make_async_copy(mask.at[me], bits.at[0], in_sem.at[2])
    load_f = pltpu.make_async_copy(mask.at[far], bits.at[1], in_sem.at[3])
    load_q.start()
    load_m.start()
    load_f.start()

    peers = [at(y, zat(dz), c, x) for dz in range(1, NZ)]
    peers += [at(yat(dy), z, core(k), x) for dy in NEAR_DY for k in range(NC) if (dy, k) != (0, 0)]
    peers += [far_device]
    peers += [at(y, z, core(k), xat(dx)) for dx in range(1, NX) for k in range(NC)]
    barrier = pltpu.get_barrier_semaphore()
    for peer in peers:
        pl.semaphore_signal(barrier, inc=1, device_id=peer, device_id_type=MESH)
    load_q.wait()
    load_e.start()
    pl.semaphore_wait(barrier, len(peers))

    ring_a = [q0, ra1, ra2, ra3]
    ring_b = [q0, rb1, rb2, rb3]
    right, left = at(y, zat(1), c, x), at(y, zat(-1), c, x)
    half = BLK_DEV // 2

    def push_ring(d):
        if d < 3:
            return (
                send(ring_a[d], ring_a[d + 1], z_send.at[0, d], z_recv.at[0, d], right),
                send(ring_b[d], ring_b[d + 1], z_send.at[1, d], z_recv.at[1, d], left),
            )
        lo, hi = pl.ds(0, half), pl.ds(half, half)
        return (
            send(ring_a[3].at[lo], r4.at[lo], z_send.at[0, 3], z_recv.at[0, 3], right),
            send(ring_b[3].at[hi], r4.at[hi], z_send.at[1, 3], z_recv.at[1, 3], left),
        )

    near_copies = {}
    far_copies = {}
    passed_on = {}

    def chosen(yy, cc, owner):
        return jnp.clip(pick[blk_id(yy, z, cc), owner], 0, BLK_DEV - 1)

    def stage(slot, ring_ref, zz):
        owner = blk_id(y, zz, c)
        held_f[zz, c] = ring_ref[chosen(yat(2), c, owner)]
        staged_f[slot] = ring_ref[chosen(yat(2), other, owner)]
        mine, theirs = held_f.at[zz, c], staged_f.at[slot]
        routes = [
            (mine, 6 + c, at(y, z, c, xat(1))),
            (mine, 2 + c, at(y, z, c, xat(3))),
            (theirs, 6 + c, at(y, z, other, xat(1))),
            (theirs, 2 + c, at(y, z, other, xat(3))),
            (theirs, c, at(y, z, other, x)),
        ]
        far_copies[slot] = [
            send(src, held_f.at[zz, place], f_send.at[slot, i], f_recv.at[slot, i], target)
            for i, (src, place, target) in enumerate(routes)
        ]
        copies = []
        for n, dy in enumerate(NEAR_DY):
            for k in range(NC):
                rows = ring_ref[chosen(yat(dy), core(k), owner)]
                if (n, k) == (0, 0):
                    held_a[zz, c] = rows
                    continue
                i = n * NC + k - 1
                staged_a[slot, i] = rows
                copies.append(send(
                    staged_a.at[slot, i], held_a.at[zz, SEEN_AS[n] * NC + c],
                    a_send.at[slot, i], a_recv.at[slot, i], at(yat(dy), z, core(k), x),
                ))
        near_copies[slot] = copies

    def forward(slot, zz):
        top, low = pl.ds(0, Q // 2), pl.ds(Q // 2, Q // 2)
        routes = [
            (0, 6 + c, 4 + c, top, xat(1)),
            (1, 2 + c, 4 + c, low, xat(3)),
            (2, 6 + other, 4 + other, top, xat(1)),
            (3, 2 + other, 4 + other, low, xat(3)),
        ]
        copies = []
        for i, place, dest, rows, xx in routes:
            far_copies[slot][i].wait_recv()
            copies.append(send(
                held_f.at[zz, place, rows], held_f.at[zz, dest, rows],
                w_send.at[slot, i], w_recv.at[slot, i], at(y, z, c, xx),
            ))
        passed_on[slot] = copies

    def own_block(a, carry):
        top = pl.multiple_of((x // 2) * LANES, LANES)
        scores = lax.dot_general(
            emb_v[a], emb_v[a, pl.ds(top, LANES), :], NT, preferred_element_type=jnp.float32,
        ) * TO_BASE2
        row = lax.broadcasted_iota(jnp.int32, (BR, LANES), 0)
        col = lax.broadcasted_iota(jnp.int32, (BR, LANES), 1) + top
        valid = (col // Q == x) & (row != col)
        row_max[a] = jnp.where(valid, scores, LOW)
        row_sum[a] = jnp.where(valid, 1.0, 0.0)
        return carry

    def prepare():
        far_max[...] = jnp.full_like(far_max, LOW)
        far_sum[...] = jnp.zeros_like(far_sum)
        row_send[...] = jnp.full_like(row_send, LOW)
        bits_wide[...] = jnp.zeros_like(bits_wide)
        load_m.wait()
        load_f.wait()
        wide = []
        for i in range(2):
            bits_wide[0:64, 0:BLK_DEV] = bits[i].astype(jnp.float32)
            wide.append(bits_wide[...].T[:8])

        def fill(zz, carry):
            p = lax.broadcasted_iota(jnp.int32, (128, COLS_A), 0)
            col = lax.broadcasted_iota(jnp.int32, (128, COLS_A), 1)
            n = col // LANES
            yy = lax.rem(y + jnp.where(n == 2, NY - 1, n), NY)
            owner = blk_id(yy, zz, lax.rem(col // Q, NC))
            live = jnp.dot(wide[0], (p == owner).astype(jnp.float32), preferred_element_type=jnp.float32)
            bias_a[zz] = jnp.where(live > 0.5, 0.0, LOW)
            p = lax.broadcasted_iota(jnp.int32, (128, COLS_F), 0)
            col = lax.broadcasted_iota(jnp.int32, (128, COLS_F), 1)
            owner = blk_id(y, zz, lax.rem(col // Q, NC))
            live = jnp.dot(wide[1], (p == owner).astype(jnp.float32), preferred_element_type=jnp.float32)
            bias_f[zz] = jnp.where(live > 0.5, 0.0, LOW)
            for n, dy in enumerate((0, 1, NY - 1, 2)):
                for cc in range(NC):
                    s = n * NC + cc
                    pcol[zz, s:s + 1, :] = jnp.full((1, 128), pick[blk_id(yat(dy), zz, cc), me], jnp.int32)
            return carry

        lax.fori_loop(0, NZ, fill, 0)
        load_e.wait()
        lax.fori_loop(0, BLK_DEV, own_block, 0)

    def absorb(t, rows, cols, row_at, sum_at):
        parts = [t[:, g * 128:(g + 1) * 128] for g in range(cols // 128)]
        old = row_at[...]
        new = old
        for part in parts:
            new = jnp.maximum(new, part)
        total = sum_at[...] * jnp.exp2(old - new)
        for part in parts:
            total += jnp.exp2(part - new)
        row_at[...] = new
        sum_at[...] = total
        t8 = t.reshape(rows // 8, 8, cols)
        old = col_max[:, :cols]
        new = jnp.maximum(old, jnp.max(t8, axis=0))
        col_sum[:, :cols] = col_sum[:, :cols] * jnp.exp2(old - new) + jnp.sum(jnp.exp2(t8 - new[None]), axis=0)
        col_max[:, :cols] = new

    def clear_cols():
        col_max[...] = jnp.full_like(col_max, LOW)
        col_sum[...] = jnp.zeros_like(col_sum)

    def finish_cols(zz, cols, dest):
        peak = jnp.max(col_max[:, :cols], axis=0, keepdims=True)
        total = jnp.sum(col_sum[:, :cols] * jnp.exp2(col_max[:, :cols] - peak), axis=0, keepdims=True)
        lse = peak + jnp.log2(total)
        for g in range(cols // 128):
            dest[g, pl.ds(zz, 1), :] = lse[:, g * 128:(g + 1) * 128]

    def compute_a(slot, zz):
        for copy in near_copies[slot]:
            copy.wait_recv()
        clear_cols()

        def one(a, carry):
            t = lax.dot_general(
                emb_v[a], held_a[zz].reshape(COLS_A, W), NT, preferred_element_type=jnp.float32,
            ) * TO_BASE2 + bias_a[zz, pl.ds(a, 1), :]
            absorb(t, BR, COLS_A, row_max.at[a], row_sum.at[a])
            return carry

        lax.fori_loop(0, BLK_DEV, one, 0)
        finish_cols(zz, COLS_A, col_send_a)

    def compute_f(slot, zz):
        far_copies[slot][4].wait_recv()
        for copy in passed_on[slot]:
            copy.wait_recv()
        clear_cols()
        far_t[...] = lax.dot_general(
            g2[...].reshape(BLK_DEV * Q, W), held_f[zz].reshape(COLS_F, W), NT,
            preferred_element_type=jnp.float32,
        ).reshape(BLK_DEV, Q, COLS_F)

        def one(a, carry):
            t = far_t[a] * TO_BASE2 + bias_f[zz, pl.ds(a, 1), :]
            absorb(t, Q, COLS_F, far_max.at[a], far_sum.at[a])
            return carry

        lax.fori_loop(0, BLK_DEV, one, 0)
        finish_cols(zz, COLS_F, col_send_f)

    ring = push_ring(0)
    stage(0, q0, z)
    far_rows = send(q0, g2, g_send, g_recv, far_device)
    prepare()
    forward(0, z)
    ready = [(0, z)]
    for d in range(1, 4):
        for copy in ring:
            copy.wait_recv()
        ring = push_ring(d)
        now = [(2 * d - 1, zat(-d)), (2 * d, zat(d))]
        stage(*now[0][:1], ring_a[d], now[0][1])
        stage(*now[1][:1], ring_b[d], now[1][1])
        for item in ready:
            compute_a(*item)
        forward(*now[0])
        if d == 1:
            far_rows.wait_recv()
        for item in ready:
            compute_f(*item)
        forward(*now[1])
        ready = now
    for copy in ring:
        copy.wait_recv()
    last = (7, zat(4))
    stage(7, r4, last[1])
    for item in ready:
        compute_a(*item)
    forward(*last)
    for item in ready:
        compute_f(*item)
    compute_a(*last)

    near_back = []
    for n, dy in enumerate(NEAR_DY):
        for k in range(NC):
            place = SEEN_AS[n] * NC + c
            if (n, k) == (0, 0):
                col_mid[place] = col_send_a[0]
                continue
            i = n * NC + k - 1
            near_back.append(send(
                col_send_a.at[n], col_mid.at[place], ca_send.at[i], ca_recv.at[i], at(yat(dy), z, core(k), x)
            ))
    compute_f(*last)
    far_back = []
    for dx in range(NX):
        for k in range(NC):
            place = (NX - dx) % NX
            if (dx, k) == (0, 0):
                col_far[c, place] = col_send_f[0]
                continue
            i = dx * NC + k - 1
            far_back.append(send(
                col_send_f.at[dx], col_far.at[c, place], cf_send.at[i], cf_recv.at[i], at(y, z, core(k), xat(dx))
            ))

    def row_lse(m, s):
        m, s = m.T, s.T
        peak = jnp.max(m, axis=0, keepdims=True)
        return peak + jnp.log2(jnp.sum(s * jnp.exp2(m - peak), axis=0, keepdims=True))

    for a in range(BLK_DEV):
        lse = row_lse(row_max[a], row_sum[a])
        for h in range(2):
            row_send[h, a:a + 1, :] = lse[:, h * 128:(h + 1) * 128]
    across = []
    for dx in range(1, NX):
        xx = xat(dx)
        across.append(send(
            row_send.at[xx // 2], row_got.at[x], x_send.at[dx - 1], x_recv.at[dx - 1], at(y, z, c, xx)
        ))
    row_got[x] = row_send[x // 2]
    for i in range(BLK_DEV // 2):
        m = far_max[2 * i:2 * i + 2].reshape(LANES, 128)
        s = far_sum[2 * i:2 * i + 2].reshape(LANES, 128)
        far_send[i:i + 1, :] = row_lse(m, s)
    far_back_rows = send(far_send, far_got, rf_send, rf_recv, far_device)

    for copy in [*near_back, *far_back]:
        copy.wait_recv()
    for cc in range(NC):
        v = [col_far[cc, i] for i in range(NX)]
        peak = jnp.maximum(jnp.maximum(v[0], v[1]), jnp.maximum(v[2], v[3]))
        total = sum(jnp.exp2(part - peak) for part in v)
        col_mid[NEAR * NC + cc] = peak + jnp.log2(total)
    for zz in range(NZ):
        for s in range(PLANE):
            col_turn[zz, s:s + 1, :] = col_mid[s, zz:zz + 1, :]
    final = []
    for dz in range(1, NZ):
        zz = zat(dz)
        final.append(send(
            col_turn.at[zz], col_got.at[z], cz_send.at[dz - 1], cz_recv.at[dz - 1], at(y, zz, c, x)
        ))
    col_got[z] = col_turn[z]
    far_back_rows.wait_recv()
    for copy in [*across, *final]:
        copy.wait_recv()

    def to_front(v, shift_it):
        return jnp.where(shift_it, pltpu.roll(v, Q, 1), v)

    got = col_got[...].reshape(NZ * PLANE, 128)
    who = pcol[...].reshape(NZ * PLANE, 128)
    for b in range(BLK_DEV):
        is_it = who == b
        v = jnp.where(is_it, got, LOW)
        peak = jnp.max(v, axis=0, keepdims=True)
        total = jnp.sum(jnp.where(is_it, jnp.exp2(v - peak), 0.0), axis=0, keepdims=True)
        col_max[b:b + 1, 0:128] = peak
        col_sum[b:b + 1, 0:128] = total
        v = far_got[b // 2:b // 2 + 1, :]
        col_max[b:b + 1, 128:256] = v if b % 2 == 0 else pltpu.roll(v, Q, 1)
    col_peak = to_front(col_max[:, 0:128], c == 1)
    col_total = to_front(col_sum[:, 0:128], c == 1)
    rows = [to_front(row_got[i], lax.rem(x, 2) == 1) for i in range(NX)]
    rows.append(col_max[:, 128:256])
    peak = col_peak
    for r in rows:
        peak = jnp.maximum(peak, r)
    total = col_total * jnp.exp2(col_peak - peak)
    for r in rows:
        total += jnp.exp2(r - peak)
    result = (peak + jnp.log2(total)) * LN2
    out[...] = result[:BLK_DEV, :Q]
    for copy in pending:
        copy.wait_send()


def body(embeddings, pick, mask):
    vmem = pl.BlockSpec(memory_space=pltpu.VMEM)
    anywhere = pl.BlockSpec(memory_space=pl.ANY)
    dma = pltpu.SemaphoreType.DMA
    f32, bf16 = jnp.float32, jnp.bfloat16
    slab = pltpu.VMEM((BLK_DEV, Q, W), bf16)
    return pl.pallas_call(
        kernel,
        out_shape=jax.ShapeDtypeStruct((BLK_DEV, Q), f32),
        in_specs=[anywhere, pl.BlockSpec(memory_space=pltpu.SMEM), anywhere],
        out_specs=vmem,
        scratch_shapes=[
            *[slab] * 9,
            pltpu.VMEM((BLK_DEV, BR, W), bf16),
            pltpu.VMEM((NZ, NEAR * NC - 1, Q, W), bf16),
            pltpu.VMEM((NZ, Q, W), bf16),
            pltpu.VMEM((NZ, NEAR * NC, Q, W), bf16),
            pltpu.VMEM((NZ, NX * NC, Q, W), bf16),
            pltpu.VMEM((2, 64, BLK_DEV), jnp.int32),
            pltpu.VMEM((128, 128), f32),
            pltpu.VMEM((NZ, 8, COLS_A), f32),
            pltpu.VMEM((NZ, 8, COLS_F), f32),
            pltpu.VMEM((NZ, PLANE, 128), jnp.int32),
            pltpu.VMEM((BLK_DEV, BR, 128), f32),
            pltpu.VMEM((BLK_DEV, BR, 128), f32),
            pltpu.VMEM((BLK_DEV, Q, 128), f32),
            pltpu.VMEM((BLK_DEV, Q, 128), f32),
            pltpu.VMEM((BLK_DEV, Q, COLS_F), f32),
            pltpu.VMEM((8, COLS_F), f32),
            pltpu.VMEM((8, COLS_F), f32),
            pltpu.VMEM((NEAR, NZ, 128), f32),
            pltpu.VMEM((NX, NZ, 128), f32),
            pltpu.VMEM((PLANE, NZ, 128), f32),
            pltpu.VMEM((NC, NX, NZ, 128), f32),
            pltpu.VMEM((NZ, PLANE, 128), f32),
            pltpu.VMEM((NZ, PLANE, 128), f32),
            pltpu.VMEM((2, 8, 128), f32),
            pltpu.VMEM((NX, 8, 128), f32),
            pltpu.VMEM((8, 128), f32),
            pltpu.VMEM((8, 128), f32),
            dma((4,)),
            dma((2, 4)), dma((2, 4)),
            dma, dma,
            dma((NZ, NEAR * NC - 1)), dma((NZ, NEAR * NC - 1)),
            dma((NZ, 5)), dma((NZ, 5)),
            dma((NZ, 4)), dma((NZ, 4)),
            dma((NEAR * NC - 1,)), dma((NEAR * NC - 1,)),
            dma((PLANE - 1,)), dma((PLANE - 1,)),
            dma((NZ - 1,)), dma((NZ - 1,)),
            dma((NX - 1,)), dma((NX - 1,)),
            dma, dma,
        ],
        compiler_params=pltpu.CompilerParams(
            collective_id=0, has_side_effects=True, vmem_limit_bytes=56 * 1024 * 1024
        ),
        cost_estimate=pl.CostEstimate(
            flops=2 * 1536 * 4096 * W, bytes_accessed=8 * 1024 * 1024, transcendentals=2 * 1536 * 4096
        ),
    )(embeddings.reshape(BLK_DEV, BR, W), pick, mask)


def solution(mesh):
    return jax.shard_map(
        body,
        mesh=mesh,
        in_specs=(P("blk", None), P(), P()),
        out_specs=P("blk", "rep"),
        check_vma=False,
    )
```

time: 129 us -> 111 us (0.86)
  Pallas kernels: 123 us -> 106 us
    pallas_call x1, Pallas kernels: 123 us -> 106 us  [body(): pl.pallas_call(kernel, out_shape=jax.ShapeDtypeStruct((BLK_DEV, Q), f32),...]
    unnamed x1 -> x2, local copies, waits for them, and re-layouts: 1.26 us -> 4.26 us
where the time goes in v2:
time: 111 us
  Pallas kernels  106 us (95%)
  local copies, waits for them, and re-layouts  4.26 us (4%)
    pallas_call x1, Pallas kernels, body(): pl.pallas_call(kernel, out_shape=jax.ShapeDtypeStruct((BLK_DEV, Q), f32),...  106 us
    unnamed x2, local copies, waits for them, and re-layouts  4.26 us

profile of v2, /device:TPU:1, one launch (start us, length us, event | category | flops | bytes accessed | tf_op | source)
XLA Modules:
  0.0 110.7 jit_solution(11592664492585250365)
XLA Ops:
  0.0 3.0 %copy.4.mask = s32[64,64,6]{2,1,0:T(8,128)} copy(s32[64,64,6]{1,0,2:T(8,128)} %param.5) | data formatting | bytes 196608 | tf_op args[2]
  3.0 106.5 %shard_map.37 = f32[6,64]{1,0:T(8,128)} custom-call(bf16[6,256,1024]{2,1,0:T(8,128)(2,1)} %bitcast.1, s32[64,64]{1,0:T(8,128)} %pick.1, s32[64,64,6]{2,1,0:T(8,128)} %copy.4.mask), custom_call_target="tpu_custom_call" | custom-call | flops 12884901888 | bytes 8388608 | tf_op jit(solution)/shard_map/pallas_call | solution.py:410
  109.5 1.3 %copy.6 = f32[6,64]{1,0:T(8,128)} copy(f32[6,64]{1,0:T(8,128)} %shard_map.37) | data formatting | bytes 3072

commit v3 on v2

v3 whole, which is shorter than its diff:
```python
import math

import jax
import jax.numpy as jnp
from jax import lax
from jax.experimental import pallas as pl
from jax.experimental.pallas import tpu as pltpu
from jax.sharding import PartitionSpec as P

W = 1024
BR = 256
BLK_DEV = 6
NY, NZ, NC, NX = 4, 8, 2, 4
PLANE = NY * NC
Q = BR // NX
LANES = NC * Q
NEAR = 3
COLS_A = NEAR * LANES
COLS_F = NX * LANES
LOW = -1e30
TO_BASE2 = math.log2(math.e) / math.sqrt(W)
LN2 = math.log(2.0)
NT = (((1,), (1,)), ((), ()))
MESH = pl.DeviceIdType.MESH
NEAR_DY = (0, 1, NY - 1)
SEEN_AS = (0, 2, 1)


def kernel(
    emb, pick_hbm, mask, out,
    pick, q0, a10, a11, a20, a21, a30, a31, b10, b11, b20, b21, b30, b31, r40, r41, g2, emb_v, staged_a, staged_f, held_a, held_f,
    bits, bits_wide, bias_a, bias_f, pcol, row_max, row_sum, far_max, far_sum, t_near, t_far, col_max, col_sum,
    col_send_a, col_send_f, col_mid, col_far, col_turn, col_got, row_send, row_got, far_send, far_got,
    in_sem, z_send, z_recv, g_send, g_recv, a_send, a_recv, f_send, f_recv, w_send, w_recv,
    ca_send, ca_recv, cf_send, cf_recv, cz_send, cz_recv, x_send, x_recv,
):
    me = lax.axis_index("blk")
    x = lax.axis_index("rep")
    c = lax.rem(me, NC)
    z = lax.rem(me // NC, NZ)
    y = me // (NC * NZ)
    other = 1 - c

    def blk_id(yy, zz, cc):
        return (yy * NZ + zz) * NC + cc

    def zat(dz):
        return lax.rem(z + dz + NZ, NZ)

    def yat(dy):
        return lax.rem(y + dy, NY)

    def xat(dx):
        return lax.rem(x + dx, NX)

    def at(yy, zz, cc, xx):
        return {"blk": blk_id(yy, zz, cc), "rep": xx}

    def core(k):
        return c if k == 0 else other

    far = blk_id(yat(2), z, c)
    far_device = at(yat(2), z, c, x)

    def send(src, dst, ssem, rsem, target):
        pltpu.make_async_remote_copy(
            src_ref=src, dst_ref=dst, send_sem=ssem, recv_sem=rsem, device_id=target, device_id_type=MESH,
        ).start()

    def await_bytes(like, sem):
        pltpu.make_async_copy(like, like, sem).wait()

    load_q = pltpu.make_async_copy(emb.at[:, pl.ds(x * Q, Q), :], q0, in_sem.at[0])
    load_e = pltpu.make_async_copy(emb, emb_v, in_sem.at[1])
    load_p = pltpu.make_async_copy(pick_hbm, pick, in_sem.at[3])
    load_m = pltpu.make_async_copy(mask, bits, in_sem.at[2])
    load_q.start()
    load_p.start()
    load_m.start()

    peers = [at(y, zat(dz), c, x) for dz in (1, -1)]
    peers += [at(yat(dy), z, core(k), x) for dy in NEAR_DY for k in range(NC) if (dy, k) != (0, 0)]
    peers += [far_device]
    peers += [at(y, z, core(k), xat(dx)) for dx in (1, NX - 1) for k in range(NC)]
    barrier = pltpu.get_barrier_semaphore()
    for peer in peers:
        pl.semaphore_signal(barrier, inc=1, device_id=peer, device_id_type=MESH)
    load_q.wait()
    load_p.wait()
    load_e.start()
    pl.semaphore_wait(barrier, len(peers))

    part = [pl.ds(0, Q // 2), pl.ds(Q // 2, Q // 2)]
    own = (q0.at[:, part[0]], q0.at[:, part[1]])
    r4 = (r40, r41)
    ring_a = [own, (a10, a11), (a20, a21), (a30, a31)]
    ring_b = [own, (b10, b11), (b20, b21), (b30, b31)]
    right, left = at(y, zat(1), c, x), at(y, zat(-1), c, x)
    def push_ring(d, h):
        for i, (chain, target) in enumerate(((ring_a, right), (ring_b, left))):
            if d < 3 or i == h:
                dst = chain[d + 1] if d < 3 else r4
                send(chain[d][h], dst[h], z_send, z_recv.at[d, h if d < 3 else 0], target)

    def await_ring(d, h):
        if d < 3:
            await_bytes(q0, z_recv.at[d, h])
        else:
            await_bytes(q0, z_recv.at[3, 0])

    def chosen(yy, cc, owner):
        return jnp.clip(pick[blk_id(yy, z, cc), owner], 0, BLK_DEV - 1)

    def stage_far(slot, ring_ref, zz, h):
        owner = blk_id(y, zz, c)
        held_f[slot, c, part[h]] = ring_ref[h][chosen(yat(2), c, owner)]
        staged_f[slot, part[h]] = ring_ref[h][chosen(yat(2), other, owner)]
        mine, theirs = held_f.at[slot, c, part[h]], staged_f.at[slot, part[h]]
        routes = [
            (mine, 6 + c, at(y, z, c, xat(1))),
            (mine, 2 + c, at(y, z, c, xat(3))),
            (theirs, 6 + c, at(y, z, other, xat(1))),
            (theirs, 2 + c, at(y, z, other, xat(3))),
            (theirs, c, at(y, z, other, x)),
        ]
        for i, (src, place, target) in enumerate(routes):
            goes_on = i < 4 and i % 2 == h
            send(
                src, held_f.at[slot, place, part[h]], f_send, f_recv.at[slot, h] if goes_on else w_recv.at[slot], target
            )

    def stage_near(slot, ring_ref, zz):
        owner = blk_id(y, zz, c)
        for n, dy in enumerate(NEAR_DY):
            for k in range(NC):
                index = chosen(yat(dy), core(k), owner)
                i = n * NC + k - 1
                for h in range(2):
                    if i < 0:
                        held_a[slot, c, part[h]] = ring_ref[h][index]
                    else:
                        staged_a[slot, i, part[h]] = ring_ref[h][index]
                if i < 0:
                    continue
                send(
                    staged_a.at[slot, i], held_a.at[slot, SEEN_AS[n] * NC + c],
                    a_send, a_recv.at[slot], at(yat(dy), z, core(k), x),
                )

    def forward(slot, zz, h):
        await_bytes(staged_f.at[slot], f_recv.at[slot, h])
        for k in range(NC):
            place = (6, 2)[h] + core(k)
            send(
                held_f.at[slot, place, part[h]], held_f.at[slot, 4 + core(k), part[h]],
                w_send, w_recv.at[slot], at(y, z, c, xat((1, 3)[h])),
            )

    def own_block(a, carry):
        top = pl.multiple_of((x // 2) * LANES, LANES)
        scores = lax.dot_general(
            emb_v[a], emb_v[a, pl.ds(top, LANES), :], NT, preferred_element_type=jnp.float32,
        ) * TO_BASE2
        row = lax.broadcasted_iota(jnp.int32, (BR, LANES), 0)
        col = lax.broadcasted_iota(jnp.int32, (BR, LANES), 1) + top
        valid = (col // Q == x) & (row != col)
        row_max[a] = jnp.where(valid, scores, LOW)
        row_sum[a] = jnp.where(valid, 1.0, 0.0)
        return carry

    def prepare():
        far_max[...] = jnp.full_like(far_max, LOW)
        far_sum[...] = jnp.zeros_like(far_sum)
        row_send[...] = jnp.full_like(row_send, LOW)
        bits_wide[...] = jnp.zeros_like(bits_wide)
        load_m.wait()
        for i, row in enumerate((me, far)):
            for a in range(BLK_DEV):
                bits_wide[i, a:a + 1, 0:64] = bits[a, pl.ds(row, 1), :].astype(jnp.float32)
        wide = [bits_wide[i] for i in range(2)]

        def fill(slot, carry):
            d = (slot + 1) // 2
            zz = lax.rem(z + d - 2 * d * lax.rem(slot, 2) + NZ, NZ)
            p = lax.broadcasted_iota(jnp.int32, (128, COLS_A), 0)
            col = lax.broadcasted_iota(jnp.int32, (128, COLS_A), 1)
            n = col // LANES
            yy = lax.rem(y + jnp.where(n == 2, NY - 1, n), NY)
            owner = blk_id(yy, zz, lax.rem(col // Q, NC))
            live = jnp.dot(wide[0], (p == owner).astype(jnp.float32), preferred_element_type=jnp.float32)
            bias_a[slot] = jnp.where(live > 0.5, 0.0, LOW)
            p = lax.broadcasted_iota(jnp.int32, (128, COLS_F), 0)
            col = lax.broadcasted_iota(jnp.int32, (128, COLS_F), 1)
            owner = blk_id(y, zz, lax.rem(col // Q, NC))
            live = jnp.dot(wide[1], (p == owner).astype(jnp.float32), preferred_element_type=jnp.float32)
            bias_f[slot] = jnp.where(live > 0.5, 0.0, LOW)
            for n, dy in enumerate((0, 1, NY - 1, 2)):
                for cc in range(NC):
                    s = n * NC + cc
                    pcol[zz, s:s + 1, :] = jnp.full((1, 128), pick[blk_id(yat(dy), zz, cc), me], jnp.int32)
            return carry

        lax.fori_loop(0, NZ, fill, 0)
        load_e.wait()
        lax.fori_loop(0, BLK_DEV, own_block, 0)

    def absorb(t, cols, row_at, sum_at):
        parts = [t[:, g * 128:(g + 1) * 128] for g in range(cols // 128)]
        old = row_at[...]
        new = old
        for p in parts:
            new = jnp.maximum(new, p)
        total = sum_at[...] * jnp.exp2(old - new)
        for p in parts:
            total += jnp.exp2(p - new)
        row_at[...] = new
        sum_at[...] = total
        t8 = t.reshape(t.shape[0] // 8, 8, cols)
        old = col_max[:, :cols]
        new = jnp.maximum(old, jnp.max(t8, axis=0))
        col_sum[:, :cols] = col_sum[:, :cols] * jnp.exp2(old - new) + jnp.sum(jnp.exp2(t8 - new[None]), axis=0)
        col_max[:, :cols] = new

    def score(items, blocks, held, bias, width, t_ref, row_at, sum_at, dest):
        first, count = items[0][0], len(items)
        cols = count * width
        col_max[...] = jnp.full_like(col_max, LOW)
        col_sum[...] = jnp.zeros_like(col_sum)

        def product(g):
            lhs = blocks[g]
            t_ref[g % 2, :lhs.shape[0], :cols] = lax.dot_general(
                lhs, held[first:first + count].reshape(cols, W), NT, preferred_element_type=jnp.float32,
            )

        def sums(g):
            per = BLK_DEV // len(blocks)
            rows = blocks[g].shape[0] // per
            for i in range(per):
                a = g * per + i
                shift = jnp.concatenate([bias[slot, a:a + 1, :] for slot, _ in items], axis=1)
                absorb(
                    t_ref[g % 2, i * rows:(i + 1) * rows, :cols] * TO_BASE2 + shift, cols, row_at.at[a], sum_at.at[a]
                )

        product(0)
        for g in range(1, len(blocks)):
            product(g)
            sums(g - 1)
        sums(len(blocks) - 1)
        peak = jnp.max(col_max[:, :cols], axis=0, keepdims=True)
        total = jnp.sum(col_sum[:, :cols] * jnp.exp2(col_max[:, :cols] - peak), axis=0, keepdims=True)
        lse = peak + jnp.log2(total)
        for n, (_, zz) in enumerate(items):
            for g in range(width // 128):
                lo = n * width + g * 128
                dest[g, pl.ds(zz, 1), :] = lse[:, lo:lo + 128]

    def compute_a(items):
        for slot, _ in items:
            await_bytes(staged_a.at[slot], a_recv.at[slot])
        blocks = [emb_v[a] for a in range(BLK_DEV)]
        score(items, blocks, held_a, bias_a, COLS_A, t_near, row_max, row_sum, col_send_a)

    def compute_f(items):
        for slot, _ in items:
            await_bytes(staged_a.at[slot], w_recv.at[slot])
        blocks = [g2[2 * g:2 * g + 2].reshape(2 * Q, W) for g in range(BLK_DEV // 2)]
        score(items, blocks, held_f, bias_f, COLS_F, t_far, far_max, far_sum, col_send_f)

    push_ring(0, 0)
    push_ring(0, 1)
    stage_far(0, own, z, 0)
    stage_far(0, own, z, 1)
    send(q0, g2, g_send, g_recv, far_device)
    stage_near(0, own, z)
    prepare()
    forward(0, z, 0)
    ready, late = [(0, z)], []
    for d in range(1, 4):
        now = [(2 * d - 1, ring_a[d], zat(-d)), (2 * d, ring_b[d], zat(d))]
        for h in range(2):
            await_ring(d - 1, h)
            push_ring(d, h)
            for item in now:
                stage_far(*item, h)
            if h == 0:
                for item in ready:
                    forward(*item, 1)
                if d == 2:
                    await_bytes(q0, g_recv)
                if late:
                    compute_f(late)
            else:
                for item in now:
                    stage_near(*item)
                now = [(slot, zz) for slot, _, zz in now]
                for item in now:
                    forward(*item, 0)
                compute_a(ready)
        ready, late = now, ready
    last = (7, zat(4))
    await_ring(3, 0)
    for h in range(2):
        stage_far(7, r4, last[1], h)
    stage_near(7, r4, last[1])
    for item in ready:
        forward(*item, 1)
    compute_f(late)
    compute_a(ready)
    forward(*last, 0)
    forward(*last, 1)
    compute_f(ready)
    compute_a([last])

    for n, dy in enumerate(NEAR_DY):
        for k in range(NC):
            place = SEEN_AS[n] * NC + c
            if (n, k) == (0, 0):
                col_mid[place] = col_send_a[0]
                continue
            send(col_send_a.at[n], col_mid.at[place], ca_send, ca_recv, at(yat(dy), z, core(k), x))
    compute_f([last])
    for dx in range(NX):
        for k in range(NC):
            place = (NX - dx) % NX
            if (dx, k) == (0, 0):
                col_far[c, place] = col_send_f[0]
                continue
            send(col_send_f.at[dx], col_far.at[c, place], cf_send, cf_recv, at(y, z, core(k), xat(dx)))

    def row_lse(m, s):
        v = (m + jnp.log2(jnp.maximum(s, 1.0))).T
        peak = jnp.max(v, axis=0, keepdims=True)
        return peak + jnp.log2(jnp.sum(jnp.exp2(v - peak), axis=0, keepdims=True))

    for a in range(BLK_DEV):
        lse = row_lse(row_max[a], row_sum[a])
        for h in range(2):
            row_send[h, a:a + 1, :] = lse[:, h * 128:(h + 1) * 128]
    for dx in range(1, NX):
        xx = xat(dx)
        send(row_send.at[xx // 2], row_got.at[x], x_send, x_recv, at(y, z, c, xx))
    row_got[x] = row_send[x // 2]
    for i in range(BLK_DEV // 2):
        m = far_max[2 * i:2 * i + 2].reshape(LANES, 128)
        s = far_sum[2 * i:2 * i + 2].reshape(LANES, 128)
        far_send[i:i + 1, :] = row_lse(m, s)
    send(far_send, far_got, x_send, x_recv, far_device)

    await_bytes(col_got.at[pl.ds(0, 5)], ca_recv)
    await_bytes(col_got.at[pl.ds(0, 7)], cf_recv)
    for cc in range(NC):
        v = [col_far[cc, i] for i in range(NX)]
        peak = jnp.maximum(jnp.maximum(v[0], v[1]), jnp.maximum(v[2], v[3]))
        total = sum(jnp.exp2(part - peak) for part in v)
        col_mid[NEAR * NC + cc] = peak + jnp.log2(total)
    for zz in range(NZ):
        for s in range(PLANE):
            col_turn[zz, s:s + 1, :] = col_mid[s, zz:zz + 1, :]
    for dz in range(1, NZ):
        zz = zat(dz)
        send(col_turn.at[zz], col_got.at[z], cz_send, cz_recv, at(y, zz, c, x))
    col_got[z] = col_turn[z]
    await_bytes(row_got, x_recv)
    await_bytes(col_turn.at[pl.ds(0, 7)], cz_recv)

    def to_front(v, shift_it):
        return jnp.where(shift_it, pltpu.roll(v, Q, 1), v)

    got = col_got[...].reshape(NZ * PLANE, 128)
    who = pcol[...].reshape(NZ * PLANE, 128)
    for b in range(BLK_DEV):
        is_it = who == b
        v = jnp.where(is_it, got, LOW)
        peak = jnp.max(v, axis=0, keepdims=True)
        total = jnp.sum(jnp.where(is_it, jnp.exp2(v - peak), 0.0), axis=0, keepdims=True)
        col_max[b:b + 1, 0:128] = peak
        col_sum[b:b + 1, 0:128] = total
        v = far_got[b // 2:b // 2 + 1, :]
        col_max[b:b + 1, 128:256] = v if b % 2 == 0 else pltpu.roll(v, Q, 1)
    col_peak = to_front(col_max[:, 0:128], c == 1)
    col_total = to_front(col_sum[:, 0:128], c == 1)
    rows = [to_front(row_got[i], lax.rem(x, 2) == 1) for i in range(NX)]
    rows.append(col_max[:, 128:256])
    peak = col_peak
    for r in rows:
        peak = jnp.maximum(peak, r)
    total = col_total * jnp.exp2(col_peak - peak)
    for r in rows:
        total += jnp.exp2(r - peak)
    result = peak + jnp.log2(total)
    out[...] = result[:BLK_DEV, :Q]
    await_bytes(held_a.at[pl.ds(0, 7)], z_send)
    await_bytes(q0, g_send)
    await_bytes(staged_a, a_send)
    await_bytes(staged_a, f_send)
    await_bytes(held_f.at[pl.ds(0, 2)], w_send)
    await_bytes(col_turn.at[pl.ds(0, 5)], ca_send)
    await_bytes(col_turn.at[pl.ds(0, 7)], cf_send)
    await_bytes(col_turn.at[pl.ds(0, 7)], cz_send)
    await_bytes(row_got, x_send)


def body(embeddings, pick, mask):
    vmem = pl.BlockSpec(memory_space=pltpu.VMEM)
    anywhere = pl.BlockSpec(memory_space=pl.ANY)
    dma = pltpu.SemaphoreType.DMA
    f32, bf16 = jnp.float32, jnp.bfloat16
    slab = pltpu.VMEM((BLK_DEV, Q, W), bf16)
    base2 = pl.pallas_call(
        kernel,
        out_shape=jax.ShapeDtypeStruct((BLK_DEV, Q), f32),
        in_specs=[anywhere, anywhere, anywhere],
        out_specs=vmem,
        scratch_shapes=[
            pltpu.SMEM((64, 64), jnp.int32),
            slab,
            *[pltpu.VMEM((BLK_DEV, Q // 2, W), bf16)] * 14,
            slab,
            pltpu.VMEM((BLK_DEV, BR, W), bf16),
            pltpu.VMEM((NZ, NEAR * NC - 1, Q, W), bf16),
            pltpu.VMEM((NZ, Q, W), bf16),
            pltpu.VMEM((NZ, NEAR * NC, Q, W), bf16),
            pltpu.VMEM((NZ, NX * NC, Q, W), bf16),
            pltpu.VMEM((BLK_DEV, 64, 64), jnp.int32),
            pltpu.VMEM((2, 8, 128), f32),
            pltpu.VMEM((NZ, 8, COLS_A), f32),
            pltpu.VMEM((NZ, 8, COLS_F), f32),
            pltpu.VMEM((NZ, PLANE, 128), jnp.int32),
            pltpu.VMEM((BLK_DEV, BR, 128), f32),
            pltpu.VMEM((BLK_DEV, BR, 128), f32),
            pltpu.VMEM((BLK_DEV, Q, 128), f32),
            pltpu.VMEM((BLK_DEV, Q, 128), f32),
            pltpu.VMEM((2, BR, 2 * COLS_A), f32),
            pltpu.VMEM((2, 2 * Q, 2 * COLS_F), f32),
            pltpu.VMEM((8, 2 * COLS_F), f32),
            pltpu.VMEM((8, 2 * COLS_F), f32),
            pltpu.VMEM((NEAR, NZ, 128), f32),
            pltpu.VMEM((NX, NZ, 128), f32),
            pltpu.VMEM((PLANE, NZ, 128), f32),
            pltpu.VMEM((NC, NX, NZ, 128), f32),
            pltpu.VMEM((NZ, PLANE, 128), f32),
            pltpu.VMEM((NZ, PLANE, 128), f32),
            pltpu.VMEM((2, 8, 128), f32),
            pltpu.VMEM((NX, 8, 128), f32),
            pltpu.VMEM((8, 128), f32),
            pltpu.VMEM((8, 128), f32),
            dma((4,)),
            dma, dma((4, 2)),
            dma, dma,
            dma, dma((NZ,)),
            dma, dma((NZ, 2)),
            dma, dma((NZ,)),
            *[dma] * 8,
        ],
        compiler_params=pltpu.CompilerParams(
            collective_id=0, has_side_effects=True, vmem_limit_bytes=56 * 1024 * 1024
        ),
        cost_estimate=pl.CostEstimate(
            flops=2 * 1536 * 4096 * W, bytes_accessed=8 * 1024 * 1024, transcendentals=2 * 1536 * 4096
        ),
    )(embeddings.reshape(BLK_DEV, BR, W), pick, mask.transpose(2, 0, 1))
    return base2 * LN2


def solution(mesh):
    return jax.shard_map(
        body,
        mesh=mesh,
        in_specs=(P("blk", None), P(), P()),
        out_specs=P("blk", "rep"),
        check_vma=False,
    )
```

time: 111 us -> 101 us (0.910)
  Pallas kernels: 106 us -> 99.9 us
  local copies, waits for them, and re-layouts: 4.26 us -> 0 us
  other arithmetic: 0 us -> 1.28 us
    pallas_call x1, Pallas kernels: 106 us -> 99.9 us  [body(): pl.pallas_call(kernel, out_shape=jax.ShapeDtypeStruct((BLK_DEV, Q), f32),...]
    unnamed x2 -> x0, local copies, waits for them, and re-layouts: 4.26 us -> none
    mul x0 -> x1, other arithmetic: none -> 1.28 us  [body(): return base2 * LN2]
where the time goes in v3:
time: 101 us
  Pallas kernels  99.9 us (99%)
  other arithmetic  1.28 us (1%)
    pallas_call x1, Pallas kernels, body(): pl.pallas_call(kernel, out_shape=jax.ShapeDtypeStruct((BLK_DEV, Q), f32),...  99.9 us

profile of v3, /device:TPU:1, one launch (start us, length us, event | category | flops | bytes accessed | tf_op | source)
XLA Modules:
  0.0 101.2 jit_solution(12476250219258632834)
XLA Ops:
  0.0 99.9 %shard_map.37 = f32[6,64]{1,0:T(8,128)} custom-call(bf16[6,256,1024]{2,1,0:T(8,128)(2,1)} %bitcast.2, s32[64,64]{1,0:T(8,128)} %pick_hbm.1, s32[6,64,64]{2,1,0:T(8,128)} %bitcast.3), custom_call_target="tpu_custom_call" | custom-call | flops 12884901888 | bytes 8388608 | tf_op jit(solution)/shard_map/pallas_call | solution.py:411
  99.9 1.3 %broadcast_multiply_fusion = f32[6,64]{1,0:T(8,128)} fusion(f32[6,64]{1,0:T(8,128)} %shard_map.37), kind=kLoop, calls=%fused_computation | loop fusion | flops 384 | bytes 3072 | tf_op jit(solution)/shard_map/mul | solution.py:464

commit v4 on v3

--- a/solution.py
+++ b/solution.py
@@ -28,11 +28,13 @@
 
 def kernel(
     emb, pick_hbm, mask, out,
-    pick, q0, a10, a11, a20, a21, a30, a31, b10, b11, b20, b21, b30, b31, r40, r41, g2, emb_v, staged_a, staged_f, held_a, held_f,
+    pick, q0, a10, a11, a20, a21, a30, a31, b10, b11, b20, b21, b30, b31, r400, r401, r410, r411, g2, emb_v, staged_a, staged_f, held_a, held_f,
     bits, bits_wide, bias_a, bias_f, pcol, row_max, row_sum, far_max, far_sum, t_near, t_far, col_max, col_sum,
     col_send_a, col_send_f, col_mid, col_far, col_turn, col_got, row_send, row_got, far_send, far_got,
+    last_a, last_f, end_near, end_far,
     in_sem, z_send, z_recv, g_send, g_recv, a_send, a_recv, f_send, f_recv, w_send, w_recv,
     ca_send, ca_recv, cf_send, cf_recv, cz_send, cz_recv, x_send, x_recv,
+    ea_send, ea_recv, ef_send, ef_recv,
 ):
     me = lax.axis_index("blk")
     x = lax.axis_index("rep")
@@ -92,30 +94,31 @@
 
     part = [pl.ds(0, Q // 2), pl.ds(Q // 2, Q // 2)]
     own = (q0.at[:, part[0]], q0.at[:, part[1]])
-    r4 = (r40, r41)
+    r4 = ((r400, r401), (r410, r411))
     ring_a = [own, (a10, a11), (a20, a21), (a30, a31)]
     ring_b = [own, (b10, b11), (b20, b21), (b30, b31)]
     right, left = at(y, zat(1), c, x), at(y, zat(-1), c, x)
-    def push_ring(d, h):
+    def push_ring(d, turn):
         for i, (chain, target) in enumerate(((ring_a, right), (ring_b, left))):
-            if d < 3 or i == h:
-                dst = chain[d + 1] if d < 3 else r4
-                send(chain[d][h], dst[h], z_send, z_recv.at[d, h if d < 3 else 0], target)
-
-    def await_ring(d, h):
-        if d < 3:
-            await_bytes(q0, z_recv.at[d, h])
-        else:
-            await_bytes(q0, z_recv.at[3, 0])
+            h = (turn + i) % 2
+            if d < 3:
+                send(chain[d][h], chain[d + 1][h], z_send, z_recv.at[d, turn], target)
+            elif turn == 0:
+                for r in range(2):
+                    send(chain[d][h].at[:, pl.ds(r * Q // 4, Q // 4)], r4[h][r], z_send, z_recv.at[d, r], target)
+
+    def await_ring(d, turn):
+        await_bytes(q0 if d < 3 else a10, z_recv.at[d, turn])
 
     def chosen(yy, cc, owner):
         return jnp.clip(pick[blk_id(yy, z, cc), owner], 0, BLK_DEV - 1)
 
-    def stage_far(slot, ring_ref, zz, h):
+    def stage_far(slot, slab, zz, h, lo, count, first):
         owner = blk_id(y, zz, c)
-        held_f[slot, c, part[h]] = ring_ref[h][chosen(yat(2), c, owner)]
-        staged_f[slot, part[h]] = ring_ref[h][chosen(yat(2), other, owner)]
-        mine, theirs = held_f.at[slot, c, part[h]], staged_f.at[slot, part[h]]
+        rows = pl.ds(lo, count)
+        held_f[slot, c, rows] = slab[chosen(yat(2), c, owner)]
+        staged_f[slot, rows] = slab[chosen(yat(2), other, owner)]
+        mine, theirs = held_f.at[slot, c, rows], staged_f.at[slot, rows]
         routes = [
             (mine, 6 + c, at(y, z, c, xat(1))),
             (mine, 2 + c, at(y, z, c, xat(3))),
@@ -123,23 +126,27 @@
             (theirs, 2 + c, at(y, z, other, xat(3))),
             (theirs, c, at(y, z, other, x)),
         ]
-        for i, (src, place, target) in enumerate(routes):
+        order = (0, 2, 1, 3, 4) if h == 0 else (1, 3, 0, 2, 4)
+        for i in order:
+            src, place, target = routes[i]
             goes_on = i < 4 and i % 2 == h
             send(
-                src, held_f.at[slot, place, part[h]], f_send, f_recv.at[slot, h] if goes_on else w_recv.at[slot], target
+                src, held_f.at[slot, place, rows], f_send, f_recv.at[first, h] if goes_on else w_recv.at[slot], target
             )
 
-    def stage_near(slot, ring_ref, zz):
+    def stage_near(slot, slabs, zz):
         owner = blk_id(y, zz, c)
         for n, dy in enumerate(NEAR_DY):
             for k in range(NC):
                 index = chosen(yat(dy), core(k), owner)
                 i = n * NC + k - 1
-                for h in range(2):
+                count = Q // len(slabs)
+                for g, slab in enumerate(slabs):
+                    rows = pl.ds(g * count, count)
                     if i < 0:
-                        held_a[slot, c, part[h]] = ring_ref[h][index]
+                        held_a[slot, c, rows] = slab[index]
                     else:
-                        staged_a[slot, i, part[h]] = ring_ref[h][index]
+                        staged_a[slot, i, rows] = slab[index]
                 if i < 0:
                     continue
                 send(
@@ -147,12 +154,13 @@
                     a_send, a_recv.at[slot], at(yat(dy), z, core(k), x),
                 )
 
-    def forward(slot, zz, h):
-        await_bytes(staged_f.at[slot], f_recv.at[slot, h])
+    def forward(slot, h, lo, count, first):
+        rows = pl.ds(lo, count)
+        await_bytes(staged_f.at[0, pl.ds(0, 2 * count)], f_recv.at[first, h])
         for k in range(NC):
             place = (6, 2)[h] + core(k)
             send(
-                held_f.at[slot, place, part[h]], held_f.at[slot, 4 + core(k), part[h]],
+                held_f.at[slot, place, rows], held_f.at[slot, 4 + core(k), rows],
                 w_send, w_recv.at[slot], at(y, z, c, xat((1, 3)[h])),
             )
 
@@ -171,7 +179,8 @@
     def prepare():
         far_max[...] = jnp.full_like(far_max, LOW)
         far_sum[...] = jnp.zeros_like(far_sum)
-        row_send[...] = jnp.full_like(row_send, LOW)
+        for ref in (row_send, far_send, col_send_a, col_send_f):
+            ref[...] = jnp.full_like(ref, LOW)
         bits_wide[...] = jnp.zeros_like(bits_wide)
         load_m.wait()
         for i, row in enumerate((me, far)):
@@ -221,7 +230,7 @@
         col_sum[:, :cols] = col_sum[:, :cols] * jnp.exp2(old - new) + jnp.sum(jnp.exp2(t8 - new[None]), axis=0)
         col_max[:, :cols] = new
 
-    def score(items, blocks, held, bias, width, t_ref, row_at, sum_at, dest):
+    def score(items, blocks, held, bias, width, t_ref, row_at, sum_at, dest, alone):
         first, count = items[0][0], len(items)
         cols = count * width
         col_max[...] = jnp.full_like(col_max, LOW)
@@ -254,85 +263,106 @@
         for n, (_, zz) in enumerate(items):
             for g in range(width // 128):
                 lo = n * width + g * 128
-                dest[g, pl.ds(zz, 1), :] = lse[:, lo:lo + 128]
-
-    def compute_a(items):
+                if not alone:
+                    dest[g, pl.ds(zz, 1), :] = lse[:, lo:lo + 128]
+                else:
+                    dest[g] = jnp.broadcast_to(lse[:, lo:lo + 128], (8, 128))
+
+    def compute_a(items, dest=col_send_a, alone=False):
         for slot, _ in items:
             await_bytes(staged_a.at[slot], a_recv.at[slot])
         blocks = [emb_v[a] for a in range(BLK_DEV)]
-        score(items, blocks, held_a, bias_a, COLS_A, t_near, row_max, row_sum, col_send_a)
-
-    def compute_f(items):
+        score(items, blocks, held_a, bias_a, COLS_A, t_near, row_max, row_sum, dest, alone)
+
+    def compute_f(items, dest=col_send_f, alone=False):
         for slot, _ in items:
             await_bytes(staged_a.at[slot], w_recv.at[slot])
         blocks = [g2[2 * g:2 * g + 2].reshape(2 * Q, W) for g in range(BLK_DEV // 2)]
-        score(items, blocks, held_f, bias_f, COLS_F, t_far, far_max, far_sum, col_send_f)
+        score(items, blocks, held_f, bias_f, COLS_F, t_far, far_max, far_sum, dest, alone)
 
     push_ring(0, 0)
     push_ring(0, 1)
-    stage_far(0, own, z, 0)
-    stage_far(0, own, z, 1)
+    for h in range(2):
+        stage_far(0, own[h], z, h, h * Q // 2, Q // 2, 0)
     send(q0, g2, g_send, g_recv, far_device)
     stage_near(0, own, z)
     prepare()
-    forward(0, z, 0)
+    forward(0, 0, 0, Q // 2, 0)
     ready, late = [(0, z)], []
     for d in range(1, 4):
-        now = [(2 * d - 1, ring_a[d], zat(-d)), (2 * d, ring_b[d], zat(d))]
-        for h in range(2):
-            await_ring(d - 1, h)
-            push_ring(d, h)
-            for item in now:
-                stage_far(*item, h)
-            if h == 0:
-                for item in ready:
-                    forward(*item, 1)
+        now = [(2 * d - 1, zat(-d)), (2 * d, zat(d))]
+        chains = [ring_a[d], ring_b[d]]
+        for turn in range(2):
+            await_ring(d - 1, turn)
+            push_ring(d, turn)
+            for i, (slot, zz) in enumerate(now):
+                h = (turn + i) % 2
+                stage_far(slot, chains[i][h], zz, h, h * Q // 2, Q // 2, slot)
+            if turn == 0:
+                if d == 1:
+                    forward(0, 1, Q // 2, Q // 2, 0)
+                    continue
+                for i, (slot, _) in enumerate(ready):
+                    h = (1 + i) % 2
+                    forward(slot, h, h * Q // 2, Q // 2, slot)
                 if d == 2:
                     await_bytes(q0, g_recv)
-                if late:
-                    compute_f(late)
+                compute_f(late)
             else:
-                for item in now:
-                    stage_near(*item)
-                now = [(slot, zz) for slot, _, zz in now]
-                for item in now:
-                    forward(*item, 0)
+                for i, (slot, zz) in enumerate(now):
+                    stage_near(slot, chains[i], zz)
+                for i, (slot, _) in enumerate(now):
+                    forward(slot, i, i * Q // 2, Q // 2, slot)
                 compute_a(ready)
         ready, late = now, ready
+    for i, (slot, _) in enumerate(ready):
+        h = (1 + i) % 2
+        forward(slot, h, h * Q // 2, Q // 2, slot)
+    compute_f(late)
     last = (7, zat(4))
-    await_ring(3, 0)
-    for h in range(2):
-        stage_far(7, r4, last[1], h)
-    stage_near(7, r4, last[1])
-    for item in ready:
-        forward(*item, 1)
-    compute_f(late)
+    rounds = [(h, h * Q // 2 + r * Q // 4, Q // 4, 7 + r) for r in range(2) for h in range(2)]
+    for r in range(2):
+        await_ring(3, r)
+        for h, lo, count, first in rounds[2 * r:2 * r + 2]:
+            stage_far(7, r4[h][r], last[1], h, lo, count, first)
+    stage_near(7, (*r4[0], *r4[1]), last[1])
     compute_a(ready)
-    forward(*last, 0)
-    forward(*last, 1)
+    for h, lo, count, first in rounds[:2]:
+        forward(7, h, lo, count, first)
     compute_f(ready)
-    compute_a([last])
+    for h, lo, count, first in rounds[2:]:
+        forward(7, h, lo, count, first)
 
     for n, dy in enumerate(NEAR_DY):
         for k in range(NC):
             place = SEEN_AS[n] * NC + c
             if (n, k) == (0, 0):
                 col_mid[place] = col_send_a[0]
-                continue
-            send(col_send_a.at[n], col_mid.at[place], ca_send, ca_recv, at(yat(dy), z, core(k), x))
-    compute_f([last])
+            else:
+                send(col_send_a.at[n], col_mid.at[place], ca_send, ca_recv, at(yat(dy), z, core(k), x))
     for dx in range(NX):
         for k in range(NC):
             place = (NX - dx) % NX
             if (dx, k) == (0, 0):
                 col_far[c, place] = col_send_f[0]
-                continue
-            send(col_send_f.at[dx], col_far.at[c, place], cf_send, cf_recv, at(y, z, core(k), xat(dx)))
+            else:
+                send(col_send_f.at[dx], col_far.at[c, place], cf_send, cf_recv, at(y, z, core(k), xat(dx)))
+
+    compute_a([last], last_a, True)
+    for n, dy in enumerate(NEAR_DY):
+        for k in range(NC):
+            send(
+                last_a.at[n], end_near.at[SEEN_AS[n] * NC + c], ea_send, ea_recv, at(yat(dy), zat(4), core(k), x)
+            )
 
     def row_lse(m, s):
         v = (m + jnp.log2(jnp.maximum(s, 1.0))).T
         peak = jnp.max(v, axis=0, keepdims=True)
         return peak + jnp.log2(jnp.sum(jnp.exp2(v - peak), axis=0, keepdims=True))
+
+    def merge(v):
+        peak = jnp.maximum(jnp.maximum(v[0], v[1]), jnp.maximum(v[2], v[3]))
+        return peak + jnp.log2(sum(jnp.exp2(p - peak) for p in v))
 
     for a in range(BLK_DEV):
         lse = row_lse(row_max[a], row_sum[a])
@@ -342,28 +372,41 @@
         xx = xat(dx)
         send(row_send.at[xx // 2], row_got.at[x], x_send, x_recv, at(y, z, c, xx))
     row_got[x] = row_send[x // 2]
+
+    await_bytes(col_got.at[pl.ds(0, 5)], ca_recv)
+    await_bytes(col_got.at[pl.ds(0, 7)], cf_recv)
+    for cc in range(NC):
+        col_mid[NEAR * NC + cc] = merge([col_far[cc, i] for i in range(NX)])
+    for zz in range(NZ):
+        for s in range(PLANE):
+            col_turn[zz, s:s + 1, :] = col_mid[s, zz:zz + 1, :]
+    for dz in (1, 2, 3, 5, 6, 7):
+        zz = zat(dz)
+        send(col_turn.at[zz], col_got.at[z], cz_send, cz_recv, at(y, zz, c, x))
+    col_got[z] = col_turn[z]
+
+    compute_f([last], last_f, True)
+    for dx in range(NX):
+        for k in range(NC):
+            send(
+                last_f.at[dx], end_far.at[c, (NX - dx) % NX], ef_send, ef_recv, at(y, zat(4), core(k), xat(dx))
+            )
     for i in range(BLK_DEV // 2):
         m = far_max[2 * i:2 * i + 2].reshape(LANES, 128)
         s = far_sum[2 * i:2 * i + 2].reshape(LANES, 128)
         far_send[i:i + 1, :] = row_lse(m, s)
     send(far_send, far_got, x_send, x_recv, far_device)
 
-    await_bytes(col_got.at[pl.ds(0, 5)], ca_recv)
-    await_bytes(col_got.at[pl.ds(0, 7)], cf_recv)
+    await_bytes(row_got, x_recv)
+    await_bytes(col_turn.at[pl.ds(0, 6)], cz_recv)
+    await_bytes(end_near, ea_recv)
+    await_bytes(end_far, ef_recv)
+    opposite = zat(4)
+    for s in range(NEAR * NC):
+        col_got[opposite, s:s + 1, :] = end_near[s, 0:1, :]
     for cc in range(NC):
-        v = [col_far[cc, i] for i in range(NX)]
-        peak = jnp.maximum(jnp.maximum(v[0], v[1]), jnp.maximum(v[2], v[3]))
-        total = sum(jnp.exp2(part - peak) for part in v)
-        col_mid[NEAR * NC + cc] = peak + jnp.log2(total)
-    for zz in range(NZ):
-        for s in range(PLANE):
-            col_turn[zz, s:s + 1, :] = col_mid[s, zz:zz + 1, :]
-    for dz in range(1, NZ):
-        zz = zat(dz)
-        send(col_turn.at[zz], col_got.at[z], cz_send, cz_recv, at(y, zz, c, x))
-    col_got[z] = col_turn[z]
-    await_bytes(row_got, x_recv)
-    await_bytes(col_turn.at[pl.ds(0, 7)], cz_recv)
+        s = NEAR * NC + cc
+        col_got[opposite, s:s + 1, :] = merge([end_far[cc, i, 0:1, :] for i in range(NX)])
 
     def to_front(v, shift_it):
         return jnp.where(shift_it, pltpu.roll(v, Q, 1), v)
@@ -398,7 +441,9 @@
     await_bytes(held_f.at[pl.ds(0, 2)], w_send)
     await_bytes(col_turn.at[pl.ds(0, 5)], ca_send)
     await_bytes(col_turn.at[pl.ds(0, 7)], cf_send)
-    await_bytes(col_turn.at[pl.ds(0, 7)], cz_send)
+    await_bytes(col_turn.at[pl.ds(0, 6)], cz_send)
+    await_bytes(end_near, ea_send)
+    await_bytes(end_far, ef_send)
     await_bytes(row_got, x_send)
 
 
@@ -416,7 +461,8 @@
         scratch_shapes=[
             pltpu.SMEM((64, 64), jnp.int32),
             slab,
-            *[pltpu.VMEM((BLK_DEV, Q // 2, W), bf16)] * 14,
+            *[pltpu.VMEM((BLK_DEV, Q // 2, W), bf16)] * 12,
+            *[pltpu.VMEM((BLK_DEV, Q // 4, W), bf16)] * 4,
             slab,
             pltpu.VMEM((BLK_DEV, BR, W), bf16),
             pltpu.VMEM((NZ, NEAR * NC - 1, Q, W), bf16),
@@ -446,13 +492,17 @@
             pltpu.VMEM((NX, 8, 128), f32),
             pltpu.VMEM((8, 128), f32),
             pltpu.VMEM((8, 128), f32),
+            pltpu.VMEM((NEAR, 8, 128), f32),
+            pltpu.VMEM((NX, 8, 128), f32),
+            pltpu.VMEM((NEAR * NC, 8, 128), f32),
+            pltpu.VMEM((NC, NX, 8, 128), f32),
             dma((4,)),
             dma, dma((4, 2)),
             dma, dma,
             dma, dma((NZ,)),
-            dma, dma((NZ, 2)),
+            dma, dma((NZ + 1, 2)),
             dma, dma((NZ,)),
-            *[dma] * 8,
+            *[dma] * 12,
         ],
         compiler_params=pltpu.CompilerParams(
             collective_id=0, has_side_effects=True, vmem_limit_bytes=56 * 1024 * 1024

time: 101 us -> 96.5 us (0.955)
  Pallas kernels: 99.9 us -> 95.1 us
    pallas_call x1, Pallas kernels: 99.9 us -> 95.1 us  [body(): pl.pallas_call(kernel, out_shape=jax.ShapeDtypeStruct((BLK_DEV, Q), f32),...]
where the time goes in v4:
time: 96.5 us; the launch traced here: 96.4 us
  Pallas kernels  95.1 us (99%)
  other arithmetic  1.28 us (1%)
    pallas_call x1, Pallas kernels, body(): pl.pallas_call(kernel, out_shape=jax.ShapeDtypeStruct((BLK_DEV, Q), f32),...  95.1 us

profile of v4, /device:TPU:1, one launch (start us, length us, event | category | flops | bytes accessed | tf_op | source)
XLA Modules:
  0.0 96.4 jit_solution(13896712605883904086)
XLA Ops:
  0.0 95.1 %shard_map.37 = f32[6,64]{1,0:T(8,128)} custom-call(bf16[6,256,1024]{2,1,0:T(8,128)(2,1)} %bitcast.2, s32[64,64]{1,0:T(8,128)} %pick_hbm.1, s32[6,64,64]{2,1,0:T(8,128)} %bitcast.3), custom_call_target="tpu_custom_call" | custom-call | flops 12884901888 | bytes 8388608 | tf_op jit(solution)/shard_map/pallas_call | solution.py:456
  95.1 1.3 %broadcast_multiply_fusion = f32[6,64]{1,0:T(8,128)} fusion(f32[6,64]{1,0:T(8,128)} %shard_map.37), kind=kLoop, calls=%fused_computation | loop fusion | flops 384 | bytes 3072 | tf_op jit(solution)/shard_map/mul | solution.py:514
